TPU v7x, 128 devices: a whole 4x4x4 slice. The times are simulated.
128 devices in a mesh: batch: 16 (over y_hi, z, core), tensor: 8 (over x, y_lo).
Axes of the slice: x: 4, y: 4 (y_hi: 2, y_lo: 2; y = y_hi * 2 + y_lo), z: 4, core: 2. Of those that a mesh axis runs over, the one named last changes fastest.
Arguments:
- tokens: bfloat16 [2, 5120, 2048], P(None, 'batch'), may hold values from -6 to 6
- target: bfloat16 [2, 5120, 2048], P(None, 'batch'), may hold values from -6 to 6
- domain_ids: int32 [2], replicated, may hold values from 0 to 3
- domain_counts: int32 [4], replicated, may hold values from 5120 to 20479
- weight_index: int32 [4], replicated, may hold values from 0 to 7
- loss_weights: float32 [8], replicated, may hold values from 0.5 to 4
- w_query: bfloat16 [2048, 2048], P('batch', 'tensor'), may hold values from -0.125 to 0.125
- w_key: bfloat16 [2048, 1024], P('batch', 'tensor'), may hold values from -0.125 to 0.125
- w_value: bfloat16 [2048, 1024], P('batch', 'tensor'), may hold values from -0.125 to 0.125
- w_gate_out: bfloat16 [2048, 2048], P('batch', 'tensor'), may hold values from -0.125 to 0.125
- w_output: bfloat16 [2048, 2048], P('tensor', 'batch'), may hold values from -1.5 to 1.5
- w_gate: bfloat16 [2048, 6144], P('batch', 'tensor'), may hold values from -0.125 to 0.125
- w_up: bfloat16 [2048, 6144], P('batch', 'tensor'), may hold values from -0.125 to 0.125
- w_down: bfloat16 [6144, 2048], P('tensor', 'batch'), may hold values from -0.078125 to 0.078125
- norm_attn: bfloat16 [2048], P('batch'), may hold values from 0.099609375 to 1.8984375
- norm_mlp: bfloat16 [2048], P('batch'), may hold values from 0.099609375 to 1.8984375
- gain_query: bfloat16 [128], P('batch'), may hold values from 0.099609375 to 1.8984375
- gain_key: bfloat16 [128], P('batch'), may hold values from 0.099609375 to 1.8984375
Outputs:
- output: bfloat16 [2, 5120, 2048], P(None, 'batch')
- grad_tokens: float32 [2, 5120, 2048], P(None, 'batch')
- grad_query: float32 [2048, 2048], P('batch', 'tensor')
- grad_key: float32 [2048, 1024], P('batch', 'tensor')
- grad_value: float32 [2048, 1024], P('batch', 'tensor')
- grad_gate_out: float32 [2048, 2048], P('batch', 'tensor')
- grad_output: float32 [2048, 2048], P('tensor', 'batch')
- grad_gate: float32 [2048, 6144], P('batch', 'tensor')
- grad_up: float32 [2048, 6144], P('batch', 'tensor')
- grad_down: float32 [6144, 2048], P('tensor', 'batch')
- grad_norm_attn: float32 [2048], P('batch')
- grad_norm_mlp: float32 [2048], P('batch')
- grad_gain_query: float32 [128], P('batch')
- grad_gain_key: float32 [128], P('batch')
All inputs are finite; a program needn't handle non-finite values.
Results may differ from a plain program's by a relative error of at most 0.03.
Values may be sent and summed in bfloat16 or wider, within the bound.
A program may use at most 256 MiB of HBM per device.

v0:
```python
import jax
import jax.numpy as jnp
from jax import lax
from jax.sharding import PartitionSpec as P

epsilon = 1e-06
rope_base = 1000000.0


def rms_scale(values, scales):
    return values * lax.rsqrt(jnp.mean(values * values, axis=-1, keepdims=True) + epsilon) * scales


def rotate(values, cosine, sine):
    half_size = values.shape[-1] // 2
    first = values[..., :half_size]
    second = values[..., half_size:]
    return jnp.concatenate(
        [first * cosine - second * sine, second * cosine + first * sine], axis=-1
    )


def head_prepare(values, scales, cosine, sine):
    head_size = scales.shape[0]
    shaped = values.reshape(values.shape[0], values.shape[1] // head_size, head_size)
    return rotate(rms_scale(shaped, scales), cosine, sine).reshape(values.shape)


def head_cols(matrix, position, head_size):
    return matrix[:, position * head_size : (position + 1) * head_size]


def head_scores(queries, key_block, allowed, scale):
    raw_scores = lax.dot_general(
        queries, key_block, (((1,), (1,)), ((), ())), preferred_element_type=jnp.float32
    )
    return jnp.where(allowed, raw_scores * scale, -jnp.inf)


def gate_apply(attended, gate_raw):
    return attended * jax.nn.sigmoid(gate_raw)


def swiglu(gate_act, up_act):
    return jax.nn.silu(gate_act) * up_act


def shards(
    tokens,
    target,
    domain_ids,
    domain_counts,
    weight_index,
    loss_weights,
    w_query,
    w_key,
    w_value,
    w_gate_out,
    w_output,
    w_gate,
    w_up,
    w_down,
    norm_attn,
    norm_mlp,
    gain_query,
    gain_key,
):
    gathered = (
        lax.all_gather(w_query, "batch", axis=0, tiled=True),
        lax.all_gather(w_key, "batch", axis=0, tiled=True),
        lax.all_gather(w_value, "batch", axis=0, tiled=True),
        lax.all_gather(w_gate_out, "batch", axis=0, tiled=True),
        lax.all_gather(w_output, "batch", axis=1, tiled=True),
        lax.all_gather(w_gate, "batch", axis=0, tiled=True),
        lax.all_gather(w_up, "batch", axis=0, tiled=True),
        lax.all_gather(w_down, "batch", axis=1, tiled=True),
        lax.all_gather(norm_attn, "batch", axis=0, tiled=True),
        lax.all_gather(norm_mlp, "batch", axis=0, tiled=True),
        lax.all_gather(gain_query, "batch", axis=0, tiled=True),
        lax.all_gather(gain_key, "batch", axis=0, tiled=True),
    )
    full_query, full_key, full_value, full_gate_out = (
        gathered[0],
        gathered[1],
        gathered[2],
        gathered[3],
    )
    full_output, full_gate, full_up, full_down = (
        gathered[4],
        gathered[5],
        gathered[6],
        gathered[7],
    )
    gain_attn = gathered[8].astype(jnp.float32)
    gain_mlp = gathered[9].astype(jnp.float32)
    gain_q = gathered[10].astype(jnp.float32)
    gain_k = gathered[11].astype(jnp.float32)
    seq_count, seq_dev, model_width = tokens.shape
    row_count = seq_count * seq_dev
    batch_count = lax.axis_size("batch")
    device_rank = lax.axis_index("batch")
    head_size = gain_q.shape[0]
    heads_local = full_query.shape[1] // head_size
    groups_local = full_key.shape[1] // head_size
    group_size = heads_local // groups_local
    seq_len = seq_dev * batch_count
    scale = head_size ** (-0.5)
    pos_local = device_rank * seq_dev + jnp.arange(seq_dev, dtype=jnp.int32)
    key_pos = jnp.arange(seq_len, dtype=jnp.int32)
    allowed = key_pos[None, :] <= pos_local[:, None]
    half_size = head_size // 2
    inverse_freq = rope_base ** (-jnp.arange(half_size, dtype=jnp.float32) / half_size)
    row_pos = jnp.tile(pos_local, seq_count).astype(jnp.float32)
    angles = row_pos[:, None] * inverse_freq[None, :]
    cosine = jnp.cos(angles)[:, None, :]
    sine = jnp.sin(angles)[:, None, :]
    inputs = tokens.reshape(row_count, model_width).astype(jnp.float32)
    normed_low = rms_scale(inputs, gain_attn).astype(jnp.bfloat16)
    query_raw = jnp.dot(normed_low, full_query, preferred_element_type=jnp.float32)
    key_raw = jnp.dot(normed_low, full_key, preferred_element_type=jnp.float32)
    value_raw = jnp.dot(normed_low, full_value, preferred_element_type=jnp.float32)
    gate_raw = jnp.dot(normed_low, full_gate_out, preferred_element_type=jnp.float32)
    query_low = head_prepare(query_raw, gain_q, cosine, sine).astype(jnp.bfloat16)
    key_low = head_prepare(key_raw, gain_k, cosine, sine).astype(jnp.bfloat16)
    value_low = value_raw.astype(jnp.bfloat16)
    key_width = key_low.shape[1]
    key_three = key_low.reshape(seq_count, seq_dev, key_width)
    value_three = value_low.reshape(seq_count, seq_dev, key_width)
    key_all, value_all = (
        lax.all_gather(key_three, "batch", axis=1, tiled=True),
        lax.all_gather(value_three, "batch", axis=1, tiled=True),
    )
    query_three = query_low.reshape(seq_count, seq_dev, query_low.shape[1])
    seq_outs = []
    log_sums = []
    for seq_index in range(seq_count):
        head_outs = []
        seq_sums = []
        for head_index in range(heads_local):
            group_index = head_index // group_size
            scores = head_scores(
                head_cols(query_three[seq_index], head_index, head_size),
                head_cols(key_all[seq_index], group_index, head_size),
                allowed,
                scale,
            )
            row_top = jnp.max(scores, axis=-1, keepdims=True)
            weights = jnp.exp(scores - row_top)
            totals = jnp.sum(weights, axis=-1, keepdims=True)
            prob_low = (weights / totals).astype(jnp.bfloat16)
            head_outs.append(
                jnp.dot(
                    prob_low,
                    head_cols(value_all[seq_index], group_index, head_size),
                    preferred_element_type=jnp.float32,
                )
            )
            seq_sums.append(row_top + jnp.log(totals))
        seq_outs.append(jnp.concatenate(head_outs, axis=1))
        log_sums.append(seq_sums)
    attended = jnp.concatenate(seq_outs, axis=0)
    gated_low = gate_apply(attended, gate_raw).astype(jnp.bfloat16)
    attn_part = jnp.dot(gated_low, full_output, preferred_element_type=jnp.float32)
    resid = inputs + lax.psum(attn_part.astype(jnp.bfloat16), "tensor").astype(jnp.float32)
    normed_mlp_low = rms_scale(resid, gain_mlp).astype(jnp.bfloat16)
    gate_act = jnp.dot(normed_mlp_low, full_gate, preferred_element_type=jnp.float32)
    up_act = jnp.dot(normed_mlp_low, full_up, preferred_element_type=jnp.float32)
    hidden_low = swiglu(gate_act, up_act).astype(jnp.bfloat16)
    down_part = jnp.dot(hidden_low, full_down, preferred_element_type=jnp.float32)
    final = resid + lax.psum(down_part.astype(jnp.bfloat16), "tensor").astype(jnp.float32)
    output = final.astype(jnp.bfloat16).reshape(seq_count, seq_dev, model_width)
    domain_range = jnp.arange(domain_counts.shape[0], dtype=jnp.int32)
    level_pick = (
        weight_index[:, None] == jnp.arange(loss_weights.shape[0], dtype=jnp.int32)[None, :]
    ).astype(jnp.float32)
    domain_factor = (
        jnp.sum(level_pick * loss_weights[None, :], axis=1)
        * seq_len
        / domain_counts.astype(jnp.float32)
    )
    seq_pick = (domain_ids[:, None] == domain_range[None, :]).astype(jnp.float32)
    seq_weight = jnp.sum(seq_pick * domain_factor[None, :], axis=1)
    grad_final = (target.astype(jnp.float32) * seq_weight[:, None, None]).reshape(
        row_count, model_width
    )
    grad_final_low = grad_final.astype(jnp.bfloat16)
    grad_down = jnp.dot(hidden_low.T, grad_final_low, preferred_element_type=jnp.float32)
    grad_hidden = jnp.dot(grad_final_low, full_down.T, preferred_element_type=jnp.float32)
    _, swiglu_back = jax.vjp(swiglu, gate_act, up_act)
    grad_gate_act, grad_up_act = swiglu_back(grad_hidden)
    grad_gate_low = grad_gate_act.astype(jnp.bfloat16)
    grad_up_low = grad_up_act.astype(jnp.bfloat16)
    grad_gate = jnp.dot(normed_mlp_low.T, grad_gate_low, preferred_element_type=jnp.float32)
    grad_up = jnp.dot(normed_mlp_low.T, grad_up_low, preferred_element_type=jnp.float32)
    mlp_input_part = jnp.dot(
        grad_gate_low, full_gate.T, preferred_element_type=jnp.float32
    ) + jnp.dot(grad_up_low, full_up.T, preferred_element_type=jnp.float32)
    grad_normed_mlp = lax.psum(mlp_input_part.astype(jnp.bfloat16), "tensor").astype(jnp.float32)
    _, mlp_norm_back = jax.vjp(rms_scale, resid, gain_mlp)
    grad_resid_norm, grad_norm_mlp = mlp_norm_back(grad_normed_mlp)
    grad_resid = grad_final + grad_resid_norm
    grad_resid_low = grad_resid.astype(jnp.bfloat16)
    grad_output = jnp.dot(gated_low.T, grad_resid_low, preferred_element_type=jnp.float32)
    grad_gated = jnp.dot(grad_resid_low, full_output.T, preferred_element_type=jnp.float32)
    _, gate_back = jax.vjp(gate_apply, attended, gate_raw)
    grad_attended, grad_gate_raw = gate_back(grad_gated)
    grad_att_low = grad_attended.astype(jnp.bfloat16)
    grad_gate_raw_low = grad_gate_raw.astype(jnp.bfloat16)
    grad_att_three = grad_att_low.reshape(seq_count, seq_dev, grad_att_low.shape[1])
    key_back, value_back = (
        lax.all_gather(key_three, "batch", axis=1, tiled=True),
        lax.all_gather(value_three, "batch", axis=1, tiled=True),
    )
    score_grads = []
    prob_lows = []
    seq_query_grads = []
    for seq_index in range(seq_count):
        seq_scores = []
        seq_probs = []
        query_grads = []
        for head_index in range(heads_local):
            group_index = head_index // group_size
            key_block = head_cols(key_back[seq_index], group_index, head_size)
            scores = head_scores(
                head_cols(query_three[seq_index], head_index, head_size), key_block, allowed, scale
            )
            probs = jnp.exp(scores - log_sums[seq_index][head_index])
            grad_probs = lax.dot_general(
                head_cols(grad_att_three[seq_index], head_index, head_size),
                head_cols(value_back[seq_index], group_index, head_size),
                (((1,), (1,)), ((), ())),
                preferred_element_type=jnp.float32,
            )
            row_dot = jnp.sum(probs * grad_probs, axis=-1, keepdims=True)
            score_grad = (probs * (grad_probs - row_dot) * scale).astype(jnp.bfloat16)
            seq_scores.append(score_grad)
            seq_probs.append(probs.astype(jnp.bfloat16))
            query_grads.append(jnp.dot(score_grad, key_block, preferred_element_type=jnp.float32))
        score_grads.append(seq_scores)
        prob_lows.append(seq_probs)
        seq_query_grads.append(jnp.concatenate(query_grads, axis=1))
    grad_query_low = jnp.concatenate(seq_query_grads, axis=0)

    def owner_term(owner_start):
        columns = []
        for seq_index in range(seq_count):
            key_total = jnp.zeros((seq_dev, head_size), jnp.float32)
            value_total = jnp.zeros((seq_dev, head_size), jnp.float32)
            for member in range(group_size):
                grad_block = lax.dynamic_slice_in_dim(
                    score_grads[seq_index][member], owner_start, seq_dev, 1
                )
                prob_block = lax.dynamic_slice_in_dim(
                    prob_lows[seq_index][member], owner_start, seq_dev, 1
                )
                key_total = key_total + lax.dot_general(
                    grad_block,
                    head_cols(query_three[seq_index], member, head_size),
                    (((0,), (0,)), ((), ())),
                    preferred_element_type=jnp.float32,
                )
                value_total = value_total + lax.dot_general(
                    prob_block,
                    head_cols(grad_att_three[seq_index], member, head_size),
                    (((0,), (0,)), ((), ())),
                    preferred_element_type=jnp.float32,
                )
            key_parts = [key_total]
            value_parts = [value_total]
            columns.extend(key_parts + value_parts)
        return jnp.concatenate(columns, axis=1)

    count = lax.axis_size("batch") * seq_dev
    owners = count // seq_dev
    starts = jnp.arange(owners, dtype=jnp.int32) * seq_dev
    stacked = lax.map(owner_term, starts)
    key_value_grads = lax.psum_scatter(
        stacked.reshape(count, stacked.shape[2]).astype(jnp.bfloat16),
        "batch",
        scatter_dimension=0,
        tiled=True,
    ).astype(jnp.float32)
    split_grads = key_value_grads.reshape(seq_dev, seq_count, 2, key_width).transpose(1, 0, 2, 3)
    grad_key_rot = split_grads[:, :, 0, :].reshape(row_count, key_width)
    value_grad_low = split_grads[:, :, 1, :].reshape(row_count, key_width).astype(jnp.bfloat16)
    _, query_back = jax.vjp(
        lambda values, scales: head_prepare(values, scales, cosine, sine), query_raw, gain_q
    )
    query_pre, grad_gain_q = query_back(grad_query_low)
    _, key_back_fn = jax.vjp(
        lambda values, scales: head_prepare(values, scales, cosine, sine), key_raw, gain_k
    )
    key_pre, grad_gain_k = key_back_fn(grad_key_rot)
    query_grad_low = query_pre.astype(jnp.bfloat16)
    key_grad_low = key_pre.astype(jnp.bfloat16)
    grad_query = jnp.dot(normed_low.T, query_grad_low, preferred_element_type=jnp.float32)
    grad_key = jnp.dot(normed_low.T, key_grad_low, preferred_element_type=jnp.float32)
    grad_value = jnp.dot(normed_low.T, value_grad_low, preferred_element_type=jnp.float32)
    grad_gate_out = jnp.dot(normed_low.T, grad_gate_raw_low, preferred_element_type=jnp.float32)
    attn_input_part = jnp.dot(query_grad_low, full_query.T, preferred_element_type=jnp.float32)
    attn_input_part = attn_input_part + jnp.dot(
        key_grad_low, full_key.T, preferred_element_type=jnp.float32
    )
    attn_input_part = attn_input_part + jnp.dot(
        value_grad_low, full_value.T, preferred_element_type=jnp.float32
    )
    attn_input_part = attn_input_part + jnp.dot(
        grad_gate_raw_low, full_gate_out.T, preferred_element_type=jnp.float32
    )
    grad_normed, gain_q_sum, gain_k_sum = (
        lax.psum(attn_input_part.astype(jnp.bfloat16), "tensor").astype(jnp.float32),
        lax.psum(grad_gain_q.astype(jnp.bfloat16), "tensor").astype(jnp.float32),
        lax.psum(grad_gain_k.astype(jnp.bfloat16), "tensor").astype(jnp.float32),
    )
    _, attn_norm_back = jax.vjp(rms_scale, inputs, gain_attn)
    grad_input_norm, grad_norm_attn = attn_norm_back(grad_normed)
    grad_tokens = (grad_resid + grad_input_norm).reshape(seq_count, seq_dev, model_width)
    summed = (
        lax.psum_scatter(
            grad_query.astype(jnp.bfloat16), "batch", scatter_dimension=0, tiled=True
        ).astype(jnp.float32),
        lax.psum_scatter(
            grad_key.astype(jnp.bfloat16), "batch", scatter_dimension=0, tiled=True
        ).astype(jnp.float32),
        lax.psum_scatter(
            grad_value.astype(jnp.bfloat16), "batch", scatter_dimension=0, tiled=True
        ).astype(jnp.float32),
        lax.psum_scatter(
            grad_gate_out.astype(jnp.bfloat16), "batch", scatter_dimension=0, tiled=True
        ).astype(jnp.float32),
        lax.psum_scatter(
            grad_output.astype(jnp.bfloat16), "batch", scatter_dimension=1, tiled=True
        ).astype(jnp.float32),
        lax.psum_scatter(
            grad_gate.astype(jnp.bfloat16), "batch", scatter_dimension=0, tiled=True
        ).astype(jnp.float32),
        lax.psum_scatter(
            grad_up.astype(jnp.bfloat16), "batch", scatter_dimension=0, tiled=True
        ).astype(jnp.float32),
        lax.psum_scatter(
            grad_down.astype(jnp.bfloat16), "batch", scatter_dimension=1, tiled=True
        ).astype(jnp.float32),
        lax.psum_scatter(
            grad_norm_attn.astype(jnp.bfloat16), "batch", scatter_dimension=0, tiled=True
        ).astype(jnp.float32),
        lax.psum_scatter(
            grad_norm_mlp.astype(jnp.bfloat16), "batch", scatter_dimension=0, tiled=True
        ).astype(jnp.float32),
        lax.psum_scatter(
            gain_q_sum.astype(jnp.bfloat16), "batch", scatter_dimension=0, tiled=True
        ).astype(jnp.float32),
        lax.psum_scatter(
            gain_k_sum.astype(jnp.bfloat16), "batch", scatter_dimension=0, tiled=True
        ).astype(jnp.float32),
    )
    return (
        output,
        grad_tokens,
        summed[0],
        summed[1],
        summed[2],
        summed[3],
        summed[4],
        summed[5],
        summed[6],
        summed[7],
        summed[8],
        summed[9],
        summed[10],
        summed[11],
    )


def solution(mesh):
    in_specs = (
        P(None, "batch", None),
        P(None, "batch", None),
        P(),
        P(),
        P(),
        P(),
        P("batch", "tensor"),
        P("batch", "tensor"),
        P("batch", "tensor"),
        P("batch", "tensor"),
        P("tensor", "batch"),
        P("batch", "tensor"),
        P("batch", "tensor"),
        P("tensor", "batch"),
        P("batch"),
        P("batch"),
        P("batch"),
        P("batch"),
    )
    out_specs = (
        P(None, "batch", None),
        P(None, "batch", None),
        P("batch", "tensor"),
        P("batch", "tensor"),
        P("batch", "tensor"),
        P("batch", "tensor"),
        P("tensor", "batch"),
        P("batch", "tensor"),
        P("batch", "tensor"),
        P("tensor", "batch"),
        P("batch"),
        P("batch"),
        P("batch"),
        P("batch"),
    )
    return jax.shard_map(shards, mesh=mesh, in_specs=in_specs, out_specs=out_specs, check_vma=False)
```

profile of v0, /device:TPU:1, one launch (start us, length us, event | category | flops | bytes accessed | tf_op | source)
XLA Modules:
  0.0 1970.2 jit_solution(1176442754244473157)
XLA Ops:
  14.1 35.5 %all-reduce.11 = (bf16[128]{0:T(256)(128)(2,1)S(1)}, bf16[128]{0:T(256)(128)(2,1)S(1)}) all-reduce(bf16[128]{0:T(256)(128)(2,1)S(1)} %dynamic-update-slice.1, bf16[128]{0:T(256)(128)(2,1)S(1)} %dynamic-update-slice), channel_id=1, replica_groups=mesh['batch'=16,'tensor'=8] {'batch'}, use_global_device_ids=true, to_apply=%add.5 | all-reduce | flops 256 | bytes 1024
  49.7 24.2 %all-gather = bf16[16,1,128]{2,1,0:T(2,128)(2,1)S(1)} all-gather(bf16[1,1,128]{2,1,0:T(2,128)(2,1)} %bitcast.225), channel_id=1, replica_groups=mesh['batch'=16,'tensor'=8] {'batch'}, dimensions={0}, use_global_device_ids=true | all-gather | bytes 4352 | tf_op jit(solution)/shard_map/all_gather | solution.py:77
  73.9 22.6 %all_gather.47 = bf16[2048,128]{1,0:T(8,128)(2,1)S(1)} all-gather(bf16[128,128]{1,0:T(8,128)(2,1)} %param.27), channel_id=1, replica_groups=mesh['batch'=16,'tensor'=8] {'batch'}, dimensions={0}, use_global_device_ids=true | all-gather | bytes 557056 | tf_op jit(solution)/shard_map/all_gather | solution.py:70
  102.1 20.7 %all_gather.50 = bf16[2048,128]{1,0:T(8,128)(2,1)S(1)} all-gather(bf16[128,128]{1,0:T(8,128)(2,1)S(1)} %copy-done.57), channel_id=1, replica_groups=mesh['batch'=16,'tensor'=8] {'batch'}, dimensions={0}, use_global_device_ids=true | all-gather | bytes 557056 | tf_op jit(solution)/shard_map/all_gather | solution.py:71
  138.0 10.5 all-gather.13.cloned.1.call-done
  166.6 33.1 %all-gather.15.cloned.1.call-done = bf16[2,5120,128]{2,1,0:T(8,128)(2,1)} async-done(((bf16[2,320,128]{2,1,0:T(8,128)(2,1)}), bf16[2,5120,128]{2,1,0:T(8,128)(2,1)}) %all-gather.15.cloned.1.call-update) | async-done | bytes 2621456 | tf_op jit(solution)/shard_map/all_gather | solution.py:131
  199.7 4.5 fusion.59
  216.2 29.4 %all-gather.17.cloned.1.call-done = bf16[2048,256]{1,0:T(8,128)(2,1)} async-done(((bf16[128,256]{1,0:T(8,128)(2,1)}), bf16[2048,256]{1,0:T(8,128)(2,1)}) %all-gather.17.cloned.1.call-update) | async-done | bytes 1048592 | tf_op jit(solution)/shard_map/all_gather | solution.py:72
  249.5 39.8 %all-gather.19.cloned.1.call-done = bf16[256,2048]{1,0:T(8,128)(2,1)} async-done(((bf16[256,128]{1,0:T(8,128)(2,1)}), bf16[256,2048]{1,0:T(8,128)(2,1)}) %all-gather.19.cloned.1.call-update) | async-done | bytes 1048592 | tf_op jit(solution)/shard_map/all_gather | solution.py:73
  295.4 24.2 %all-gather.1 = bf16[16,1,128]{2,1,0:T(2,128)(2,1)S(1)} all-gather(bf16[1,1,128]{2,1,0:T(2,128)(2,1)S(1)} %bitcast.226), channel_id=1, replica_groups=mesh['batch'=16,'tensor'=8] {'batch'}, dimensions={0}, use_global_device_ids=true | all-gather | bytes 4352 | tf_op jit(solution)/shard_map/all_gather | solution.py:78
  326.7 88.6 %all-reduce.18.cloned.1.call-done = bf16[640,2048]{1,0:T(8,128)(2,1)} async-done(((bf16[640,2048]{1,0:T(8,128)(2,1)}), bf16[640,2048]{1,0:T(8,128)(2,1)}) %all-reduce.18.cloned.1.call-update) | async-done | bytes 2621456 | tf_op jit(solution)/shard_map/psum | solution.py:164
  421.1 49.7 %all-gather.23.cloned.1.call-done = bf16[2048,768]{1,0:T(8,128)(2,1)} async-done(((bf16[128,768]{1,0:T(8,128)(2,1)}), bf16[2048,768]{1,0:T(8,128)(2,1)}) %all-gather.23.cloned.1.call-update) | async-done | bytes 3145744 | tf_op jit(solution)/shard_map/all_gather | solution.py:75
  470.8 6.1 fusion.120
  477.0 45.9 %all-gather.21.cloned.1.call-done = bf16[2048,768]{1,0:T(8,128)(2,1)} async-done(((bf16[128,768]{1,0:T(8,128)(2,1)}), bf16[2048,768]{1,0:T(8,128)(2,1)}) %all-gather.21.cloned.1.call-update) | async-done | bytes 3145744 | tf_op jit(solution)/shard_map/all_gather | solution.py:74
  522.9 6.2 fusion.119
  529.1 46.8 %all-gather.25.cloned.1.call-done = bf16[768,2048]{1,0:T(8,128)(2,1)} async-done(((bf16[768,128]{1,0:T(8,128)(2,1)}), bf16[768,2048]{1,0:T(8,128)(2,1)}) %all-gather.25.cloned.1.call-update) | async-done | bytes 3145744 | tf_op jit(solution)/shard_map/all_gather | solution.py:76
  575.8 7.8 multiply_convert_fusion.5
  586.2 4.2 add_convert_fusion.1
  592.9 117.4 %all-reduce.20.cloned.1.call-done = bf16[640,2048]{1,0:T(8,128)(2,1)} async-done(((bf16[640,2048]{1,0:T(8,128)(2,1)}), bf16[640,2048]{1,0:T(8,128)(2,1)}) %all-reduce.20.cloned.1.call-update) | async-done | bytes 2621456 | tf_op jit(solution)/shard_map/psum | solution.py:198
  710.4 4.7 fusion.43
  715.2 4.7 fusion.45
  723.7 3.9 multiply_reduce_fusion
  727.6 3.9 multiply_reduce_fusion.1
  731.6 15.1 fusion.54
  750.7 6.8 multiply_reduce_fusion.3
  757.5 12.6 fusion.52
  770.1 236.3 %while.10 = (s32[]{:T(128)}, bf16[16,320,512]{2,1,0:T(8,128)(2,1)}, s32[16]{0:T(128)S(1)}, bf16[320,5120]{1,0:T(8,128)(2,1)}, bf16[2,320,256]{2,1,0:T(8,128)(2,1...) while((s32[]{:T(128)}, bf16[16,320,512]{2,1,0:T(8,128)(2,1)}, ...), condition=%wide.region_24.25_spmd, body=%wide.region_23.24_spmd.sunk | while | flops 211353600 | bytes 6226159 | solution.py:276
  1007.3 4.5 convolution_convert_fusion.5
  1035.9 6.3 convolution_convert_fusion
  1042.2 4.7 copy.62
  1047.0 6.3 convolution_convert_fusion.1
  1053.3 6.4 convolution_convert_fusion.2
  1060.0 5.9 convolution_convert_fusion.3
  1065.9 26.0 %reduce-scatter.14.cloned.1.call-done = bf16[320,512]{1,0:T(8,128)(2,1)} async-done(((bf16[5120,512]{1,0:T(8,128)(2,1)}), bf16[320,512]{1,0:T(8,128)(2,1)}) %reduce-scatter.14.cloned.1.call-update) | async-done | bytes 327696 | tf_op jit(solution)/shard_map/reduce_scatter | solution.py:277
  1103.8 4.5 fusion.124
  1116.5 5.2 add_convert_fusion
  1123.0 37.8 %reduce-scatter.28.cloned.1.call-done = bf16[128,256]{1,0:T(8,128)(2,1)} async-done(((bf16[2048,256]{1,0:T(8,128)(2,1)}), bf16[128,256]{1,0:T(8,128)(2,1)}) %reduce-scatter.28.cloned.1.call-update) | async-done | bytes 65552
  1162.4 68.6 %reduce-scatter.22.cloned.1.call-done = bf16[128,256]{1,0:T(8,128)(2,1)} async-done(((bf16[2048,256]{1,0:T(8,128)(2,1)}), bf16[128,256]{1,0:T(8,128)(2,1)}) %reduce-scatter.22.cloned.1.call-update) | async-done | bytes 65552 | tf_op jit(solution)/shard_map/reduce_scatter | solution.py:328
  1232.5 68.1 %reduce-scatter.16.cloned.1.call-done = bf16[128,256]{1,0:T(8,128)(2,1)} async-done(((bf16[2048,256]{1,0:T(8,128)(2,1)}), bf16[128,256]{1,0:T(8,128)(2,1)}) %reduce-scatter.16.cloned.1.call-update) | async-done | bytes 65552 | tf_op jit(solution)/shard_map/reduce_scatter | solution.py:319
  1302.1 78.1 %reduce-scatter.30.cloned.1.call-done = bf16[128,768]{1,0:T(8,128)(2,1)} async-done(((bf16[2048,768]{1,0:T(8,128)(2,1)}), bf16[128,768]{1,0:T(8,128)(2,1)}) %reduce-scatter.30.cloned.1.call-update) | async-done | bytes 196624
  1382.1 76.9 %reduce-scatter.26.cloned.1.call-done = bf16[128,768]{1,0:T(8,128)(2,1)} async-done(((bf16[2048,768]{1,0:T(8,128)(2,1)}), bf16[128,768]{1,0:T(8,128)(2,1)}) %reduce-scatter.26.cloned.1.call-update) | async-done | bytes 196624 | tf_op jit(solution)/shard_map/reduce_scatter | solution.py:337
  1460.7 77.0 %reduce-scatter.24.cloned.1.call-done = bf16[128,768]{1,0:T(8,128)(2,1)} async-done(((bf16[2048,768]{1,0:T(8,128)(2,1)}), bf16[128,768]{1,0:T(8,128)(2,1)}) %reduce-scatter.24.cloned.1.call-update) | async-done | bytes 196624 | tf_op jit(solution)/shard_map/reduce_scatter | solution.py:334
  1539.4 66.1 %reduce-scatter.18.cloned.1.call-done = bf16[128,128]{1,0:T(8,128)(2,1)} async-done(((bf16[2048,128]{1,0:T(8,128)(2,1)}), bf16[128,128]{1,0:T(8,128)(2,1)}) %reduce-scatter.18.cloned.1.call-update) | async-done | bytes 32784 | tf_op jit(solution)/shard_map/reduce_scatter | solution.py:322
  1606.9 66.9 %reduce-scatter.20.cloned.1.call-done = bf16[128,128]{1,0:T(8,128)(2,1)} async-done(((bf16[2048,128]{1,0:T(8,128)(2,1)}), bf16[128,128]{1,0:T(8,128)(2,1)}) %reduce-scatter.20.cloned.1.call-update) | async-done | bytes 32784 | tf_op jit(solution)/shard_map/reduce_scatter | solution.py:325
  1675.2 224.5 %all-reduce.22.cloned.1.call-done = (bf16[640,2048]{1,0:T(8,128)(2,1)}, bf16[640,2048]{1,0:T(8,128)(2,1)}) async-done(((bf16[640,2048]{1,0:T(8,128)(2,1)}, bf16[640,2048]{1,0:T(8,128)(2,1)}), (bf16[640,2048]{1,0:T(8,128)(2,1)}, bf16[640,2048]{1,0:T(8,128)(2,1)})) %all-reduce.22.cloned.1.call-update) | async-done | bytes 5242896 | tf_op jit(solution)/shard_map/psum | solution.py:170
  1903.5 34.1 %all-reduce.10 = (bf16[2048]{0:T(1024)(128)(2,1)S(1)}, bf16[2048]{0:T(1024)(128)(2,1)S(1)}, bf16[128]{0:T(256)(128)(2,1)S(1)}, bf16[128]{0:T(256)(128)(2,1)S(1)}) all-reduce(bf16[2048]{0:T(1024)(128)(2,1)S(1)} %get-tuple-element.97, ...), channel_id=11, replica_groups=mesh['batch'=16,'tensor'=8] {'batch'}, use_global_device_ids=true, to_apply=%region_38.39.clone | all-reduce | flops 4352 | bytes 17408
  1938.9 14.6 all-reduce.12
  1954.6 8.3 fusion.46
  (507 shorter events, 358.4 us)
Async XLA Ops:
  7.2 89.3 %copy-start = (bf16[2,320,2048]{2,1,0:T(8,128)(2,1)S(1)}, bf16[2,320,2048]{2,1,0:T(8,128)(2,1)}, u32[]{:S(2)}) copy-start(bf16[2,320,2048]{2,1,0:T(8,128)(2,1)} %param.20) | copy-start | bytes 7864324
  7.2 123.9 %all-gather.11.cloned.1.call-start = ((), (), s32[]{:S(2)}) async-start(), calls=%async_computation.9 | async-start | bytes 1114112 | tf_op jit(solution)/shard_map/all_gather | solution.py:69
  7.9 140.6 %all-gather.13.cloned.1.call-start = ((), (), s32[]{:S(2)}) async-start(), calls=%async_computation.10 | async-start | bytes 2785280 | tf_op jit(solution)/shard_map/all_gather | solution.py:130
  10.3 117.8 %copy-start.62 = (f32[64]{0:T(128)}, f32[64]{0:T(128)S(1)}, u32[]{:S(2)}) copy-start(f32[64]{0:T(128)S(1)} %multiply_power_fusion) | copy-start | bytes 772
  49.5 50.2 %copy-start.64 = (f32[128]{0:T(128)}, f32[128]{0:T(128)S(1)}, u32[]{:S(2)}) copy-start(f32[128]{0:T(128)S(1)} %convert_element_type.279) | copy-start | bytes 1540
  49.6 78.6 %copy-start.47 = (f32[640]{0:T(1024)}, f32[640]{0:T(1024)S(1)}, u32[]{:S(2)}) copy-start(f32[640]{0:T(1024)S(1)} %convert_element_type.275) | copy-start | bytes 7684
  49.7 50.0 %copy-start.55 = (f32[640]{0:T(1024)}, f32[640]{0:T(1024)S(1)}, u32[]{:S(2)}) copy-start(f32[640]{0:T(1024)S(1)} %add.211) | copy-start | bytes 7684
  49.7 50.0 %copy-start.51 = (f32[640]{0:T(1024)}, f32[640]{0:T(1024)S(1)}, u32[]{:S(2)}) copy-start(f32[640]{0:T(1024)S(1)} %rsqrt.50) | copy-start | bytes 7684
  73.9 55.0 %copy-start.40 = (f32[16,1,128]{2,1,0:T(1,128)}, f32[16,1,128]{2,1,0:T(1,128)S(1)}, u32[]{:S(2)}) copy-start(f32[16,1,128]{2,1,0:T(1,128)S(1)} %convert_element_type.349) | copy-start | bytes 24580
  102.1 97.6 %all-gather.15.cloned.1.call-start = ((), (), s32[]{:S(2)}) async-start(), calls=%async_computation.11 | async-start | bytes 2785280 | tf_op jit(solution)/shard_map/all_gather | solution.py:131
  126.9 118.7 %all-gather.17.cloned.1.call-start = ((), (), s32[]{:S(2)}) async-start(), calls=%async_computation.12 | async-start | bytes 1114112 | tf_op jit(solution)/shard_map/all_gather | solution.py:72
  127.5 161.9 %all-gather.19.cloned.1.call-start = ((), (), s32[]{:S(2)}) async-start(), calls=%async_computation.13 | async-start | bytes 1114112 | tf_op jit(solution)/shard_map/all_gather | solution.py:73
  128.1 287.2 %all-reduce.18.cloned.1.call-start = ((), (), s32[]{:S(2)}) async-start(), calls=%async_computation.14 | async-start | bytes 5242880 | tf_op jit(solution)/shard_map/psum | solution.py:164
  128.8 9.0 copy-start.34
  128.8 9.0 copy-start.36
  128.9 8.0 copy-start.60
  249.5 43.6 %copy-start.37 = (bf16[640,256]{1,0:T(8,128)(2,1)}, bf16[640,256]{1,0:T(8,128)(2,1)S(1)}, u32[]{:S(2)}) copy-start(bf16[640,256]{1,0:T(8,128)(2,1)S(1)} %get-tuple-element.188) | copy-start | bytes 983044
  289.4 30.2 %copy-start.72 = (f32[8]{0:T(128)S(1)}, f32[8]{0:T(128)}, u32[]{:S(2)}) copy-start(f32[8]{0:T(128)} %param.25) | copy-start | bytes 100
  289.4 30.2 %copy-start.73 = (s32[4]{0:T(128)S(1)}, s32[4]{0:T(128)}, u32[]{:S(2)}) copy-start(s32[4]{0:T(128)} %param.24) | copy-start | bytes 52
  289.4 30.4 %copy-start.74 = (s32[4]{0:T(128)S(1)}, s32[4]{0:T(128)}, u32[]{:S(2)}) copy-start(s32[4]{0:T(128)} %param.23) | copy-start | bytes 52
  289.4 30.4 %copy-start.75 = (s32[2]{0:T(128)S(1)}, s32[2]{0:T(128)}, u32[]{:S(2)}) copy-start(s32[2]{0:T(128)} %param.22) | copy-start | bytes 28
  293.1 177.7 %all-gather.23.cloned.1.call-start = ((), (), s32[]{:S(2)}) async-start(), calls=%async_computation.16 | async-start | bytes 3342336 | tf_op jit(solution)/shard_map/all_gather | solution.py:75
  293.8 229.0 %all-gather.21.cloned.1.call-start = ((), (), s32[]{:S(2)}) async-start(), calls=%async_computation.15 | async-start | bytes 3342336 | tf_op jit(solution)/shard_map/all_gather | solution.py:74
  294.6 281.2 %all-gather.25.cloned.1.call-start = ((), (), s32[]{:S(2)}) async-start(), calls=%async_computation.17 | async-start | bytes 3342336 | tf_op jit(solution)/shard_map/all_gather | solution.py:76
  295.3 415.1 %all-reduce.20.cloned.1.call-start = ((), (), s32[]{:S(2)}) async-start(), calls=%async_computation.18 | async-start | bytes 5242880 | tf_op jit(solution)/shard_map/psum | solution.py:198
  575.8 7.8 copy-start.68
  590.4 501.5 %reduce-scatter.14.cloned.1.call-start = ((), (), s32[]{:S(2)}) async-start(), calls=%async_computation.19 | async-start | bytes 5570560 | tf_op jit(solution)/shard_map/reduce_scatter | solution.py:277
  710.4 12.3 slice-start.2
  727.6 19.1 slice-start
  731.6 15.1 slice-start.1
  1006.4 154.4 %reduce-scatter.28.cloned.1.call-start = ((), (), s32[]{:S(2)}) async-start(), calls=%async_computation.26 | async-start | bytes 1114112
  1014.0 216.9 %reduce-scatter.22.cloned.1.call-start = ((), (), s32[]{:S(2)}) async-start(), calls=%async_computation.23 | async-start | bytes 1114112 | tf_op jit(solution)/shard_map/reduce_scatter | solution.py:328
  1018.0 282.7 %reduce-scatter.16.cloned.1.call-start = ((), (), s32[]{:S(2)}) async-start(), calls=%async_computation.20 | async-start | bytes 1114112 | tf_op jit(solution)/shard_map/reduce_scatter | solution.py:319
  1035.6 344.6 %reduce-scatter.30.cloned.1.call-start = ((), (), s32[]{:S(2)}) async-start(), calls=%async_computation.27 | async-start | bytes 3342336
  1046.9 412.1 %reduce-scatter.26.cloned.1.call-start = ((), (), s32[]{:S(2)}) async-start(), calls=%async_computation.25 | async-start | bytes 3342336 | tf_op jit(solution)/shard_map/reduce_scatter | solution.py:337
  1053.3 484.5 %reduce-scatter.24.cloned.1.call-start = ((), (), s32[]{:S(2)}) async-start(), calls=%async_computation.24 | async-start | bytes 3342336 | tf_op jit(solution)/shard_map/reduce_scatter | solution.py:334
  1059.7 545.8 %reduce-scatter.18.cloned.1.call-start = ((), (), s32[]{:S(2)}) async-start(), calls=%async_computation.21 | async-start | bytes 557056 | tf_op jit(solution)/shard_map/reduce_scatter | solution.py:322
  1065.9 32.4 %copy-start.48 = (f32[640]{0:T(1024)S(1)}, f32[640]{0:T(1024)}, u32[]{:S(2)}) copy-start(f32[640]{0:T(1024)} %copy-done.47) | copy-start | bytes 7684
  1065.9 32.4 %copy-start.63 = (f32[64]{0:T(128)S(1)}, f32[64]{0:T(128)}, u32[]{:S(2)}) copy-start(f32[64]{0:T(128)} %copy-done.62) | copy-start | bytes 772
  1065.9 34.0 %copy-start.22 = (f32[640,128]{0,1:T(8,128)S(1)}, f32[640,128]{0,1:T(8,128)}, u32[]{:S(2)}) copy-start(f32[640,128]{0,1:T(8,128)} %copy-done.21) | copy-start | bytes 983044
  1065.9 34.0 %copy-start.50 = (f32[640]{0:T(1024)S(1)}, f32[640]{0:T(1024)}, u32[]{:S(2)}) copy-start(f32[640]{0:T(1024)} %copy-done.49) | copy-start | bytes 7684
  1065.9 34.0 %copy-start.65 = (f32[128]{0:T(128)S(1)}, f32[128]{0:T(128)}, u32[]{:S(2)}) copy-start(f32[128]{0:T(128)} %copy-done.64) | copy-start | bytes 1540
  1065.9 34.1 %copy-start.54 = (f32[640]{0:T(1024)S(1)}, f32[640]{0:T(1024)}, u32[]{:S(2)}) copy-start(f32[640]{0:T(1024)} %copy-done.53) | copy-start | bytes 7684
  1103.7 570.1 %reduce-scatter.20.cloned.1.call-start = ((), (), s32[]{:S(2)}) async-start(), calls=%async_computation.22 | async-start | bytes 557056 | tf_op jit(solution)/shard_map/reduce_scatter | solution.py:325
  1113.8 786.0 %all-reduce.22.cloned.1.call-start = ((), (), s32[]{:S(2)}) async-start(), calls=%async_computation.28 | async-start | bytes 10485760 | tf_op jit(solution)/shard_map/psum | solution.py:170
  1121.7 778.1 %copy-start.41 = (f32[16,1,128]{2,1,0:T(1,128)S(1)}, f32[16,1,128]{2,1,0:T(1,128)}, u32[]{:S(2)}) copy-start(f32[16,1,128]{2,1,0:T(1,128)} %copy-done.40) | copy-start | bytes 24580
  1121.7 778.1 %copy-start.52 = (f32[640]{0:T(1024)S(1)}, f32[640]{0:T(1024)}, u32[]{:S(2)}) copy-start(f32[640]{0:T(1024)} %copy-done.51) | copy-start | bytes 7684
  1382.1 521.4 %copy-start.56 = (f32[640]{0:T(1024)S(1)}, f32[640]{0:T(1024)}, u32[]{:S(2)}) copy-start(f32[640]{0:T(1024)} %copy-done.55) | copy-start | bytes 7684
  (58 other events, 199.8 us)
Sparse Core Ops, SparseCore 0:
  10.5 48.5 all-gather.10
  102.2 46.2 all-gather.12
  151.6 47.9 all-gather.14
  202.0 43.6 all-gather.16
  247.8 41.5 all-gather.18
  293.2 122.0 all-reduce.17
  417.8 52.9 all-gather.22
  473.3 49.5 all-gather.20
  525.1 50.6 all-gather.24
  590.5 119.7 all-reduce.19
  1006.5 85.4 reduce-scatter.13
  1095.6 65.1 reduce-scatter.27
  1165.0 65.9 reduce-scatter.21
  1234.6 65.9 reduce-scatter.15
  1305.0 75.1 reduce-scatter.29
  1384.7 74.2 reduce-scatter.25
  1463.4 74.2 reduce-scatter.23
  1541.7 63.7 reduce-scatter.17
  1609.2 64.5 reduce-scatter.19
  1677.0 222.7 all-reduce.21
where the time goes:
time: 1990 us; the launch traced here: 1970 us
  waiting for transfers between devices  1260 us (63%)
  matrix products  322 us (16%)
  blocking collectives  176 us (9%)
  other arithmetic  101 us (5%)
  local copies, waits for them, and re-layouts  63.3 us (3%)
  loops' own time  34.1 us (2%)
    psum x1, waiting for transfers between devices, shards(): lax.psum(down_part.astype(jnp.bfloat16), 'tensor').astype(jnp.float32)  225 us
    unnamed x22, waiting for transfers between devices  120 us
    psum x1, waiting for transfers between devices, shards(): lax.psum(mlp_input_part.astype(jnp.bfloat16), 'tensor').astype(jnp.float32)  117 us
    dot_general x64, matrix products, owner_term(): lax.dot_general(prob_block, head_cols(grad_att_three[seq_index], member,...  89.2 us
    dot_general x64, matrix products, owner_term(): lax.dot_general(grad_block, head_cols(query_three[seq_index], member, hea...  89.2 us
    psum x1, waiting for transfers between devices, shards(): lax.psum(attn_part.astype(jnp.bfloat16), 'tensor').astype(jnp.float32)  88.6 us
    reduce_scatter x1, waiting for transfers between devices, shards(): lax.psum_scatter(grad_gate.astype(jnp.bfloat16), 'batch', scatter_dimensi...  77 us
    reduce_scatter x1, waiting for transfers between devices, shards(): lax.psum_scatter(grad_up.astype(jnp.bfloat16), 'batch', scatter_dimension...  76.9 us
  transfers between devices with their start and end apart: 20, of which 19 were waited for; matrix products, arithmetic and copies ran while one was open for 9% of the time, Pallas kernels for 0%

commit v1 on v0

v1 whole, which is shorter than its diff:
```python
import functools
import math

import jax
import jax.numpy as jnp
from jax import lax
from jax.experimental import pallas as pl
from jax.experimental.pallas import tpu as pltpu
from jax.sharding import PartitionSpec as P

MESH = pl.DeviceIdType.MESH
epsilon = 1e-06
rope_base = 1000000.0
f32 = jnp.float32
bf16 = jnp.bfloat16
MIB = 2**20
ANY = pl.BlockSpec(memory_space=pl.ANY)
VM = pl.BlockSpec(memory_space=pltpu.VMEM)


class Group:
    def __init__(self, kind):
        b = lax.axis_index("batch")
        t = lax.axis_index("tensor")
        if kind == "tensor":
            r, q = lax.div(t, 2), lax.rem(t, 2)
            self.slot = lambda dr, dq: lax.rem(r + dr, 4) * 2 + lax.rem(q + dq, 2)
            at = lambda dr, dq: (b, self.slot(dr, dq))
            self.core = None
        else:
            c = lax.rem(b, 2)
            q, r = lax.div(b, 8), lax.rem(lax.div(b, 2), 4)
            self.slot = lambda dr, dq, dc=0: (
                lax.rem(q + dq, 2) * 4 + lax.rem(r + dr, 4)
            ) * 2 + lax.rem(c + dc, 2)
            at = lambda dr, dq: (self.slot(dr, dq), t)
            self.core = (self.slot(0, 0, 1), t)
        self.right, self.left, self.mate = at(1, 0), at(3, 0), at(0, 1)

    def neighbours(self):
        near = [self.right, self.left, self.mate]
        return near + ([self.core] if self.core is not None else [])


def enter(groups):
    barrier = pltpu.get_barrier_semaphore()
    near = [device for group in groups for device in group.neighbours()]
    for device in near:
        pl.semaphore_signal(barrier, inc=1, device_id=device, device_id_type=MESH)
    pl.semaphore_wait(barrier, len(near))


class Copies:
    def __init__(self, send_sem, recv_sem, local_sem):
        self.send_sem, self.recv_sem, self.local_sem = send_sem, recv_sem, local_sem
        self.count = 0
        self.locals = 0

    def send(self, source, target, device):
        copy = pltpu.make_async_remote_copy(
            src_ref=source,
            dst_ref=target,
            send_sem=self.send_sem.at[self.count],
            recv_sem=self.recv_sem.at[self.count],
            device_id=device,
            device_id_type=MESH,
        )
        self.count += 1
        copy.start()
        return copy

    def local(self, source, target):
        copy = pltpu.make_async_copy(source, target, self.local_sem.at[self.locals])
        self.locals += 1
        copy.start()
        return copy


def half_of(ref, which):
    width = ref.shape[-1] // 2
    return ref.at[:, pl.ds(which * width, width)]


def run_all(*steps):
    waiting = list(steps)
    while waiting:
        for step in list(waiting):
            try:
                next(step)
            except StopIteration:
                waiting.remove(step)


def gather(copies, group, own, slot, split=True):
    s = group.slot
    core_copies = []
    sent = []

    def push(ref, *devices):
        out = [copies.send(ref, ref, device) for device in devices]
        sent.extend(out)
        return out

    def to_core(ref):
        if group.core is not None:
            core_copies.extend(push(ref, group.core))

    home = slot(s(0, 0))
    first = [copies.send(own, home, d) for d in (group.right, group.left, group.mate)]
    sent.extend(first)
    if group.core is not None:
        core_copies.append(copies.send(own, home, group.core))
        sent.append(core_copies[0])
    kept = copies.local(own, home)
    from_left, from_right, from_mate = first
    yield
    from_left.wait_recv()
    left_unit = slot(s(3, 0))
    far = push(half_of(left_unit, 0) if split else left_unit, group.right)
    to_core(left_unit)
    from_right.wait_recv()
    right_unit = slot(s(1, 0))
    if split:
        far += push(half_of(right_unit, 1), group.left)
    to_core(right_unit)
    from_mate.wait_recv()
    mate_unit = slot(s(0, 1))
    mate_left, mate_right = push(mate_unit, group.right, group.left)
    to_core(mate_unit)
    yield
    mate_left.wait_recv()
    left_unit = slot(s(3, 1))
    mate_far = push(half_of(left_unit, 0) if split else left_unit, group.right)
    to_core(left_unit)
    mate_right.wait_recv()
    right_unit = slot(s(1, 1))
    if split:
        mate_far += push(half_of(right_unit, 1), group.left)
    to_core(right_unit)
    yield
    for copy in far:
        copy.wait_recv()
    to_core(slot(s(2, 0)))
    yield
    for copy in mate_far:
        copy.wait_recv()
    to_core(slot(s(2, 1)))
    yield
    for copy in core_copies:
        copy.wait_recv()
    for copy in sent:
        copy.wait_send()
    kept.wait()


def add_rows(target, sources, step=16):
    rows = target.shape[0]

    def body(i, carry):
        at = pl.ds(pl.multiple_of(i * step, step), step)
        total = sources[0][at, :].astype(f32)
        for source in sources[1:]:
            total = total + source[at, :].astype(f32)
        target[at, :] = total.astype(target.dtype)
        return carry

    lax.fori_loop(0, rows // step, body, 0)


def reduce_scratch(rows, width, core):
    unit = pltpu.VMEM((4, rows, width), bf16)
    shapes = [
        pltpu.VMEM((4, rows, width // 2), bf16),
        unit,
        unit,
        pltpu.VMEM((2, rows, width), bf16),
    ]
    if core:
        shapes += [
            pltpu.VMEM((8, rows, width), bf16),
            pltpu.VMEM((2, rows, width), bf16),
        ]
    return shapes


def reduce(copies, group, part, scratch, result):
    far, near, outgoing, mates = scratch[:4]
    core = group.core is not None
    sent = []

    def send(source, target, device):
        copy = copies.send(source, target, device)
        sent.append(copy)
        return copy

    order = [(2, 1), (2, 0), (1, 1), (3, 1), (1, 0), (3, 0), (0, 1), (0, 0)]
    arrived = {}
    if core:
        from_core, far_units = scratch[4:]
        for n, (dr, dq) in enumerate(order):
            arrived[dr, dq] = (send(part(dr, dq, 1), from_core.at[n], group.core), n)
        yield

    def terms(dr, dq):
        if not core:
            return [part(dr, dq)]
        copy, n = arrived[dr, dq]
        copy.wait_recv()
        return [part(dr, dq, 0), from_core.at[n]]

    far_copies = {}
    for dq in (1, 0):
        unit = terms(2, dq)
        if core:
            add_rows(far_units.at[dq], unit)
            unit = [far_units.at[dq]]
        far_copies[dq, 0] = send(half_of(unit[0], 0), far.at[dq * 2], group.right)
        far_copies[dq, 1] = send(half_of(unit[0], 1), far.at[dq * 2 + 1], group.left)
    yield
    near_copies = {}
    for dq in (1, 0):
        for way, (dr, device) in enumerate(((1, group.right), (3, group.left))):
            unit = terms(dr, dq)
            far_copies[dq, way].wait_recv()
            held = outgoing.at[dq * 2 + way]
            there = far.at[dq * 2 + way]
            add_rows(half_of(held, way), [half_of(u, way) for u in unit] + [there])
            add_rows(half_of(held, 1 - way), [half_of(u, 1 - way) for u in unit])
            near_copies[dq, way] = send(held, near.at[dq * 2 + way], device)
        yield
    unit = terms(0, 1)
    for way in (0, 1):
        near_copies[1, way].wait_recv()
    add_rows(mates.at[0], unit + [near.at[2], near.at[3]])
    to_mate = send(mates.at[0], mates.at[1], group.mate)
    yield
    unit = terms(0, 0)
    for way in (0, 1):
        near_copies[0, way].wait_recv()
    to_mate.wait_recv()
    add_rows(result, unit + [near.at[0], near.at[1], mates.at[1]])
    for copy in sent:
        copy.wait_send()


def sems(remote, local):
    return [
        pltpu.SemaphoreType.DMA((remote,)),
        pltpu.SemaphoreType.DMA((remote,)),
        pltpu.SemaphoreType.DMA((max(local, 1),)),
    ]


def params(collective, limit=48):
    return pltpu.CompilerParams(
        collective_id=collective, has_side_effects=True, vmem_limit_bytes=limit * MIB
    )


def batch_gather_kernel(count, *refs):
    own, out = refs[:count], refs[count : 2 * count]
    copies = Copies(*refs[2 * count :])
    group = Group("batch")
    enter([group])
    run_all(
        *[
            gather(copies, group, own[n], functools.partial(lambda o, s: o.at[s], out[n]), n == 0)
            for n in range(count)
        ]
    )


def batch_gather(name, collective, *arrays):
    count = len(arrays)
    return pl.pallas_call(
        functools.partial(batch_gather_kernel, count),
        out_shape=[jax.ShapeDtypeStruct((16,) + a.shape, a.dtype) for a in arrays],
        in_specs=[ANY] * count,
        out_specs=[ANY] * count,
        scratch_shapes=sems(24 * count, count),
        name=name,
        compiler_params=params(collective, 16),
    )(*arrays)


def forward_kernel(scale, q_ref, kv_ref, out_ref, sum_ref, acc_ref):
    b = lax.axis_index("batch")
    seqs, rows, head = q_ref.shape
    seq_dev = kv_ref.shape[1] // seqs
    factor = scale * math.log2(math.e)
    ones = jnp.ones((2 * seq_dev, head), bf16)
    last = lax.div(b, 2)
    tile = rows // 4
    for s in range(seqs):
        at = pl.ds(s * seq_dev, seq_dev)

        def block(pair, masked):
            first, second = pair * 2, pair * 2 + 1
            keys = jnp.concatenate([kv_ref[first, at, :head], kv_ref[second, at, :head]], axis=0)
            values = jnp.concatenate([kv_ref[first, at, head:], kv_ref[second, at, head:]], axis=0)
            wide = jnp.concatenate([values, ones], axis=1)
            for i in range(4):
                here = pl.ds(i * tile, tile)
                scores = lax.dot_general(
                    q_ref[s, here, :], keys, (((1,), (1,)), ((), ())), preferred_element_type=f32
                )
                weights = jnp.exp2(scores * factor)
                if masked:
                    row = lax.broadcasted_iota(jnp.int32, scores.shape, 0) + (i * tile) % seq_dev
                    col = lax.broadcasted_iota(jnp.int32, scores.shape, 1)
                    weights = jnp.where(col + first * seq_dev <= row + b * seq_dev, weights, 0.0)
                acc_ref[here, :] += jnp.dot(weights.astype(bf16), wide, preferred_element_type=f32)

        acc_ref[...] = jnp.zeros_like(acc_ref)

        def body(pair, carry):
            block(pair, False)
            return carry

        lax.fori_loop(0, last, body, 0)
        block(last, True)
        out_ref[s] = acc_ref[:, :head] / acc_ref[:, head:]
        sum_ref[s] = acc_ref[:, head:]


def attention_forward(queries, kv_all, scale):
    shape = jax.ShapeDtypeStruct(queries.shape, f32)
    return pl.pallas_call(
        functools.partial(forward_kernel, scale),
        out_shape=[shape, shape],
        in_specs=[VM, VM],
        out_specs=[VM, VM],
        scratch_shapes=[pltpu.VMEM((queries.shape[1], 2 * queries.shape[2]), f32)],
        name="attention_forward",
        compiler_params=pltpu.CompilerParams(vmem_limit_bytes=40 * MIB),
    )(queries, kv_all)


def backward_kernel(
    scale, q_ref, qt_ref, do_ref, dot_ref, lse_ref, delta_ref, kv_ref, dq_ref, dkv_ref, acc_ref
):
    b = lax.axis_index("batch")
    seqs, rows, head = q_ref.shape
    slots, both, _ = kv_ref.shape
    seq_dev = both // seqs
    factor = scale * math.log2(math.e)

    def clear(slot, carry):
        dkv_ref[slot] = jnp.zeros(dkv_ref.shape[1:], dkv_ref.dtype)
        return carry

    lax.fori_loop(b + 1, slots, clear, 0)
    for s in range(seqs):
        at = pl.ds(s * seq_dev, seq_dev)

        def block(slot, masked):
            keys = kv_ref[slot, at, :head]
            values = kv_ref[slot, at, head:]
            scores = jnp.dot(keys, qt_ref[s], preferred_element_type=f32)
            probs = jnp.exp2(scores * factor - lse_ref[s])
            if masked:
                key = lax.broadcasted_iota(jnp.int32, scores.shape, 0)
                col = lax.broadcasted_iota(jnp.int32, scores.shape, 1)
                row = jnp.where(col >= seq_dev, col - seq_dev, col)
                probs = jnp.where(key <= row, probs, 0.0)
            grad_probs = jnp.dot(values, dot_ref[s], preferred_element_type=f32)
            grad_scores = (probs * (grad_probs - delta_ref[s]) * scale).astype(bf16)
            dkv_ref[slot, at, :head] = jnp.dot(
                grad_scores, q_ref[s], preferred_element_type=f32
            ).astype(bf16)
            dkv_ref[slot, at, head:] = jnp.dot(
                probs.astype(bf16), do_ref[s], preferred_element_type=f32
            ).astype(bf16)
            acc_ref[...] += lax.dot_general(
                keys, grad_scores, (((0,), (0,)), ((), ())), preferred_element_type=f32
            )

        acc_ref[...] = jnp.zeros_like(acc_ref)

        def body(slot, carry):
            block(slot, False)
            return carry

        lax.fori_loop(0, b, body, 0)
        block(b, True)
        dq_ref[s] = acc_ref[...].T


def attention_backward(queries, grad_att, lse, delta, kv_all, scale):
    return pl.pallas_call(
        functools.partial(backward_kernel, scale),
        out_shape=[
            jax.ShapeDtypeStruct(queries.shape, f32),
            jax.ShapeDtypeStruct(kv_all.shape, bf16),
        ],
        in_specs=[VM] * 7,
        out_specs=[VM] * 2,
        scratch_shapes=[pltpu.VMEM((queries.shape[2], queries.shape[1]), f32)],
        name="attention_backward",
        compiler_params=pltpu.CompilerParams(vmem_limit_bytes=48 * MIB),
    )(
        queries,
        queries.transpose(0, 2, 1),
        grad_att,
        grad_att.transpose(0, 2, 1),
        lse,
        delta,
        kv_all,
    )


def rows_at(i, step=16):
    return pl.ds(pl.multiple_of(i * step, step), step)


def residual_kernel(
    part, inputs, gain, pack_a, pack_b, pack_c, normed, resid, wide_a, wide_b, wide_c, *rest
):
    scratch, own, (send_sem, recv_sem, local_sem) = rest[:4], rest[4], rest[5:]
    copies = Copies(send_sem, recv_sem, local_sem)
    tensor, batch = Group("tensor"), Group("batch")
    rows = resid.shape[0]
    enter([tensor, batch])

    def along():
        def unit(dr, dq):
            return part.at[pl.ds(pl.multiple_of(tensor.slot(dr, dq) * rows, 16), rows), :]

        yield from reduce(copies, tensor, unit, scratch, resid)

        def body(i, carry):
            at = rows_at(i)
            total = inputs[at, :] + resid[at, :]
            resid[at, :] = total
            mean = jnp.mean(total * total, axis=-1, keepdims=True)
            own[at, :] = (total * lax.rsqrt(mean + epsilon) * gain[...]).astype(bf16)
            return carry

        lax.fori_loop(0, rows // 16, body, 0)
        yield from gather(
            copies,
            tensor,
            own,
            lambda s: normed.at[pl.ds(pl.multiple_of(s * rows, 16), rows), :],
        )

    run_all(
        gather(copies, batch, pack_a, lambda s: wide_a.at[s]),
        gather(copies, batch, pack_b, lambda s: wide_b.at[s]),
        gather(copies, batch, pack_c, lambda s: wide_c.at[s]),
        along(),
    )


def residual(part, inputs, gain, packs):
    rows, width = inputs.shape
    return pl.pallas_call(
        residual_kernel,
        out_shape=[
            jax.ShapeDtypeStruct(part.shape, bf16),
            jax.ShapeDtypeStruct(inputs.shape, f32),
        ]
        + [jax.ShapeDtypeStruct((16,) + p.shape, bf16) for p in packs],
        in_specs=[VM] * 3 + [ANY] * len(packs),
        out_specs=[ANY, VM] + [ANY] * len(packs),
        scratch_shapes=reduce_scratch(rows, width, False)
        + [pltpu.VMEM((rows, width), bf16)]
        + sems(24 * 5, 5),
        name="residual_and_weights",
        compiler_params=params(3, 40),
    )(part, inputs, gain, *packs)


def norm_back(values, gain, grad):
    inverse = lax.rsqrt(jnp.mean(values * values, axis=-1, keepdims=True) + epsilon)
    scaled = grad * gain
    unit = values * inverse
    inner = jnp.mean(scaled * unit, axis=-1, keepdims=True)
    return (scaled - unit * inner) * inverse, grad * unit


def mlp_back_kernel(
    part, resid, grad_final, gain, weight_part, low, grad_resid, gain_grad, weight_grad, *rest
):
    scratch, scratch_w = rest[:4], rest[4:10]
    own, total = rest[10], rest[11]
    copies = Copies(*rest[12:])
    tensor, batch = Group("tensor"), Group("batch")
    rows = resid.shape[0]
    depth = weight_grad.shape[0]
    enter([tensor, batch])

    def along():
        def unit(dr, dq):
            return part.at[pl.ds(pl.multiple_of(tensor.slot(dr, dq) * rows, 16), rows), :]

        yield from reduce(copies, tensor, unit, scratch, grad_resid)
        total[...] = jnp.zeros_like(total)

        def body(i, carry):
            at = rows_at(i)
            back, terms = norm_back(resid[at, :], gain[...], grad_resid[at, :])
            back = grad_final[at, :] + back
            total[...] += terms
            grad_resid[at, :] = back
            own[at, :] = back.astype(bf16)
            return carry

        lax.fori_loop(0, rows // 16, body, 0)
        gain_grad[...] = jnp.sum(total[...], axis=0, keepdims=True)
        yield from gather(
            copies, tensor, own, lambda s: low.at[pl.ds(pl.multiple_of(s * rows, 16), rows), :]
        )

    def weight_unit(dr, dq, dc):
        return weight_part.at[
            pl.ds(pl.multiple_of(batch.slot(dr, dq, dc) * depth, 16), depth), :
        ]

    run_all(reduce(copies, batch, weight_unit, scratch_w, weight_grad), along())


def mlp_back(part, resid, grad_final, gain, weight_part):
    rows, width = resid.shape
    depth, columns = weight_part.shape[0] // 16, weight_part.shape[1]
    return pl.pallas_call(
        mlp_back_kernel,
        out_shape=[
            jax.ShapeDtypeStruct(part.shape, bf16),
            jax.ShapeDtypeStruct(resid.shape, f32),
            jax.ShapeDtypeStruct((1, width), f32),
            jax.ShapeDtypeStruct((depth, columns), f32),
        ],
        in_specs=[VM] * 5,
        out_specs=[ANY, VM, VM, VM],
        scratch_shapes=reduce_scratch(rows, width, False)
        + reduce_scratch(depth, columns, True)
        + [pltpu.VMEM((rows, width), bf16), pltpu.VMEM((16, width), f32)]
        + sems(24 * 3, 1),
        name="mlp_grad_and_weights",
        compiler_params=params(4, 56),
    )(part, resid, grad_final, gain, weight_part)


def output_kernel(part, resid, kv_part, output, kv_grad, *rest):
    scratch, scratch_kv = rest[:4], rest[4:10]
    own, final = rest[10], rest[11]
    copies = Copies(*rest[12:])
    tensor, batch = Group("tensor"), Group("batch")
    rows = resid.shape[0]
    enter([tensor, batch])

    def along():
        def unit(dr, dq):
            return part.at[pl.ds(pl.multiple_of(tensor.slot(dr, dq) * rows, 16), rows), :]

        yield from reduce(copies, tensor, unit, scratch, final)
        add_rows(own, [final, resid])
        yield from gather(
            copies, tensor, own, lambda s: output.at[pl.ds(pl.multiple_of(s * rows, 16), rows), :]
        )

    run_all(
        reduce(
            copies,
            batch,
            lambda dr, dq, dc: kv_part.at[batch.slot(dr, dq, dc)],
            scratch_kv,
            kv_grad,
        ),
        along(),
    )


def output_and_kv(part, resid, kv_part):
    rows, width = resid.shape
    return pl.pallas_call(
        output_kernel,
        out_shape=[
            jax.ShapeDtypeStruct(part.shape, bf16),
            jax.ShapeDtypeStruct(kv_part.shape[1:], f32),
        ],
        in_specs=[VM] * 3,
        out_specs=[ANY, VM],
        scratch_shapes=reduce_scratch(rows, width, False)
        + reduce_scratch(kv_part.shape[1], kv_part.shape[2], True)
        + [pltpu.VMEM((rows, width), bf16), pltpu.VMEM((rows, width), f32)]
        + sems(24 * 3, 1),
        name="output_and_kv_grads",
        compiler_params=params(5, 48),
    )(part, resid, kv_part)


def last_kernel(
    part, inputs, grad_resid, gain, gain_terms, weight_part, tokens, weight_grad, sums, *rest
):
    scratch, scratch_w = rest[:4], rest[4:10]
    own, held, total, mine, over_tensor, mine_too, over_batch = rest[10:17]
    copies = Copies(*rest[17:])
    tensor, batch = Group("tensor"), Group("batch")
    rows, width = inputs.shape
    depth = weight_grad.shape[0]
    enter([tensor, batch])

    def small():
        yield from gather(copies, tensor, mine, lambda s: over_tensor.at[s], False)
        total_t = over_tensor[0]
        for n in range(1, 8):
            total_t = total_t + over_tensor[n]
        mine_too[...] = total_t
        yield from gather(copies, batch, mine_too, lambda s: over_batch.at[s], False)
        total_b = over_batch[0]
        for n in range(1, 16):
            total_b = total_b + over_batch[n]
        sums[...] = total_b

    def along():
        def unit(dr, dq):
            return part.at[pl.ds(pl.multiple_of(tensor.slot(dr, dq) * rows, 16), rows), :]

        yield from reduce(copies, tensor, unit, scratch, held)
        total[...] = jnp.zeros_like(total)

        def body(i, carry):
            at = rows_at(i)
            back, terms = norm_back(inputs[at, :], gain[...], held[at, :])
            total[...] += terms
            own[at, :] = (grad_resid[at, :] + back).astype(bf16)
            return carry

        lax.fori_loop(0, rows // 16, body, 0)
        gain_row = jnp.sum(total[...], axis=0, keepdims=True)
        mine[...] = gain_terms[...]
        for n in range(width // 128):
            mine[pl.ds(n, 1), :] = gain_row[:, n * 128 : (n + 1) * 128]
        big = gather(
            copies, tensor, own, lambda s: tokens.at[pl.ds(pl.multiple_of(s * rows, 16), rows), :]
        )
        few = small()
        for _ in big:
            next(few, None)
            yield
        yield from few

    def weight_unit(dr, dq, dc):
        return weight_part.at[
            pl.ds(pl.multiple_of(batch.slot(dr, dq, dc) * depth, 16), depth), :
        ]

    run_all(reduce(copies, batch, weight_unit, scratch_w, weight_grad), along())


def last_step(part, inputs, grad_resid, gain, gain_terms, weight_part):
    rows, width = inputs.shape
    depth, columns = weight_part.shape[0] // 16, weight_part.shape[1]
    few = gain_terms.shape
    return pl.pallas_call(
        last_kernel,
        out_shape=[
            jax.ShapeDtypeStruct(part.shape, bf16),
            jax.ShapeDtypeStruct((depth, columns), f32),
            jax.ShapeDtypeStruct(few, f32),
        ],
        in_specs=[VM] * 6,
        out_specs=[ANY, VM, VM],
        scratch_shapes=reduce_scratch(rows, width, False)
        + reduce_scratch(depth, columns, True)
        + [
            pltpu.VMEM((rows, width), bf16),
            pltpu.VMEM((rows, width), f32),
            pltpu.VMEM((16, width), f32),
            pltpu.VMEM(few, f32),
            pltpu.VMEM((8,) + few, f32),
            pltpu.VMEM(few, f32),
            pltpu.VMEM((16,) + few, f32),
        ]
        + sems(24 * 5, 3),
        name="input_grad_and_weights",
        compiler_params=params(6, 48),
    )(part, inputs, grad_resid, gain, gain_terms, weight_part)


def rms_scale(values, scales):
    return values * lax.rsqrt(jnp.mean(values * values, axis=-1, keepdims=True) + epsilon) * scales


def rotate(values, cosine, sine):
    half_size = values.shape[-1] // 2
    first = values[..., :half_size]
    second = values[..., half_size:]
    return jnp.concatenate(
        [first * cosine - second * sine, second * cosine + first * sine], axis=-1
    )


def head_prepare(values, scales, cosine, sine):
    head_size = scales.shape[0]
    shaped = values.reshape(values.shape[0], values.shape[1] // head_size, head_size)
    return rotate(rms_scale(shaped, scales), cosine, sine).reshape(values.shape)


def gate_apply(attended, gate_raw):
    return attended * jax.nn.sigmoid(gate_raw)


def swiglu(gate_act, up_act):
    return jax.nn.silu(gate_act) * up_act


def dot(left, right):
    return jnp.dot(left, right, preferred_element_type=f32)


def dot_t(left, right):
    return lax.dot_general(left, right, (((1,), (1,)), ((), ())), preferred_element_type=f32)


def t_dot(left, right):
    return lax.dot_general(left, right, (((0,), (0,)), ((), ())), preferred_element_type=f32)


def shards(
    tokens,
    target,
    domain_ids,
    domain_counts,
    weight_index,
    loss_weights,
    w_query,
    w_key,
    w_value,
    w_gate_out,
    w_output,
    w_gate,
    w_up,
    w_down,
    norm_attn,
    norm_mlp,
    gain_query,
    gain_key,
):
    seq_count, seq_dev, width = tokens.shape
    rows = seq_count * seq_dev
    members = lax.axis_size("tensor")
    batch_count = lax.axis_size("batch")
    b, t = lax.axis_index("batch"), lax.axis_index("tensor")
    own_rows = rows // members
    seq_len = seq_dev * batch_count
    head = gain_query.shape[0] * batch_count
    scale = head ** (-0.5)
    q_cols, k_cols = w_query.shape[1], w_key.shape[1]
    heads = q_cols // head

    pack_attn = jnp.concatenate([w_query, w_key, w_value, w_gate_out, w_output.T], axis=1)
    few = jnp.zeros((16, norm_attn.shape[0]), bf16)
    few = few.at[0].set(norm_attn).at[1].set(norm_mlp)
    few = few.at[2, : gain_query.shape[0]].set(gain_query)
    few = few.at[3, : gain_key.shape[0]].set(gain_key)
    wide_attn, wide_few = batch_gather("attention_weights", 1, pack_attn, few)
    wide_attn = wide_attn.reshape(width, pack_attn.shape[1])
    proj_cols = 2 * q_cols + 2 * k_cols
    w_proj = wide_attn[:, :proj_cols]
    w_out_t = wide_attn[:, proj_cols:]
    gain_attn = wide_few[:, 0].reshape(1, width).astype(f32)
    gain_mlp = wide_few[:, 1].reshape(1, width).astype(f32)
    gain_q = wide_few[:, 2, : gain_query.shape[0]].reshape(head).astype(f32)
    gain_k = wide_few[:, 3, : gain_key.shape[0]].reshape(head).astype(f32)

    half_size = head // 2
    pos_local = b * seq_dev + jnp.arange(seq_dev, dtype=jnp.int32)
    inverse_freq = rope_base ** (-jnp.arange(half_size, dtype=f32) / half_size)
    row_pos = jnp.tile(pos_local, seq_count).astype(f32)
    angles = row_pos[:, None] * inverse_freq[None, :]
    cosine = jnp.cos(angles)[:, None, :]
    sine = jnp.sin(angles)[:, None, :]

    tokens_low = tokens.reshape(rows, width)
    normed_low = rms_scale(tokens_low.astype(f32), gain_attn).astype(bf16)
    proj = dot(normed_low, w_proj)
    query_raw = proj[:, :q_cols]
    key_raw = proj[:, q_cols : q_cols + k_cols]
    value_raw = proj[:, q_cols + k_cols : q_cols + 2 * k_cols]
    gate_raw = proj[:, q_cols + 2 * k_cols :]

    def prepare(values, scales):
        return head_prepare(values, scales, cosine, sine)

    query_low = prepare(query_raw, gain_q).astype(bf16)
    key_low = prepare(key_raw, gain_k).astype(bf16)
    kv_own = jnp.concatenate([key_low, value_raw.astype(bf16)], axis=1)
    (kv_all,) = batch_gather("keys_and_values", 2, kv_own)

    def by_head(values):
        shaped = values.reshape(seq_count, seq_dev, heads, head)
        return shaped.transpose(0, 2, 1, 3).reshape(seq_count, heads * seq_dev, head)

    def by_row(values):
        shaped = values.reshape(seq_count, heads, seq_dev, head)
        return shaped.transpose(0, 2, 1, 3).reshape(rows, heads * head)

    queries = by_head(query_low)
    attended_heads, sums = attention_forward(queries, kv_all, scale)
    attended = by_row(attended_heads)
    lse = jnp.log2(sums[:, :, 0])[:, None, :]
    gated_low = gate_apply(attended, gate_raw).astype(bf16)
    attn_part = dot_t(gated_low, w_out_t).astype(bf16)

    inputs_own = lax.dynamic_slice_in_dim(tokens_low, t * own_rows, own_rows, 0).astype(f32)
    packs = (w_gate, w_up, w_down.T)
    normed_mlp_low, resid_own, wide_gate, wide_up, wide_down = residual(
        attn_part, inputs_own, gain_mlp, packs
    )
    ff = w_gate.shape[1]
    wide_gate, wide_up, wide_down = (
        w.reshape(width, ff) for w in (wide_gate, wide_up, wide_down)
    )

    domain_range = jnp.arange(domain_counts.shape[0], dtype=jnp.int32)
    level_pick = (
        weight_index[:, None] == jnp.arange(loss_weights.shape[0], dtype=jnp.int32)[None, :]
    ).astype(f32)
    domain_factor = (
        jnp.sum(level_pick * loss_weights[None, :], axis=1) * seq_len / domain_counts.astype(f32)
    )
    seq_pick = (domain_ids[:, None] == domain_range[None, :]).astype(f32)
    seq_weight = jnp.sum(seq_pick * domain_factor[None, :], axis=1)
    row_weight = jnp.repeat(seq_weight, seq_dev)[:, None]
    target_low = target.reshape(rows, width)
    grad_final_low = (target_low.astype(f32) * row_weight).astype(bf16)
    grad_final_own = lax.dynamic_slice_in_dim(target_low, t * own_rows, own_rows, 0).astype(
        f32
    ) * lax.dynamic_slice_in_dim(row_weight, t * own_rows, own_rows, 0)

    gate_act = dot(normed_mlp_low, wide_gate)
    up_act = dot(normed_mlp_low, wide_up)
    hidden_low = swiglu(gate_act, up_act).astype(bf16)
    down_part = dot_t(hidden_low, wide_down).astype(bf16)
    grad_hidden = dot(grad_final_low, wide_down)
    _, swiglu_back = jax.vjp(swiglu, gate_act, up_act)
    grad_gate_act, grad_up_act = swiglu_back(grad_hidden)
    grad_gate_low = grad_gate_act.astype(bf16)
    grad_up_low = grad_up_act.astype(bf16)
    mlp_input_part = (dot_t(grad_gate_low, wide_gate) + dot_t(grad_up_low, wide_up)).astype(bf16)
    mlp_weight_part = jnp.concatenate(
        [
            t_dot(normed_mlp_low, grad_gate_low).astype(bf16),
            t_dot(normed_mlp_low, grad_up_low).astype(bf16),
            t_dot(grad_final_low, hidden_low).astype(bf16),
        ],
        axis=1,
    )
    grad_resid_low, grad_resid_own, norm_mlp_terms, mlp_weight_grad = mlp_back(
        mlp_input_part, resid_own, grad_final_own, gain_mlp, mlp_weight_part
    )

    grad_gated = dot(grad_resid_low, w_out_t)
    _, gate_back = jax.vjp(gate_apply, attended, gate_raw)
    grad_attended, grad_gate_raw = gate_back(grad_gated)
    grad_att_low = grad_attended.astype(bf16)
    grad_gate_raw_low = grad_gate_raw.astype(bf16)
    grad_att_heads = by_head(grad_att_low)
    delta = jnp.sum(grad_att_heads.astype(f32) * attended_heads, axis=-1)[:, None, :]
    grad_query_heads, kv_part = attention_backward(
        queries, grad_att_heads, lse, delta, kv_all, scale
    )
    output, kv_grad = output_and_kv(down_part, resid_own, kv_part)

    _, query_back = jax.vjp(prepare, query_raw, gain_q)
    query_pre, grad_gain_q = query_back(by_row(grad_query_heads))
    _, key_back = jax.vjp(prepare, key_raw, gain_k)
    key_pre, grad_gain_k = key_back(kv_grad[:, :k_cols])
    proj_grad_low = jnp.concatenate(
        [
            query_pre.astype(bf16),
            key_pre.astype(bf16),
            kv_grad[:, k_cols:].astype(bf16),
            grad_gate_raw_low,
        ],
        axis=1,
    )
    attn_input_part = dot_t(proj_grad_low, w_proj).astype(bf16)
    attn_weight_part = jnp.concatenate(
        [
            t_dot(normed_low, proj_grad_low).astype(bf16),
            t_dot(grad_resid_low, gated_low).astype(bf16),
        ],
        axis=1,
    )
    norm_rows = width // 128
    gain_terms = jnp.zeros((2 * norm_rows + 8, 128), f32)
    gain_terms = gain_terms.at[norm_rows : 2 * norm_rows].set(norm_mlp_terms.reshape(norm_rows, 128))
    gain_terms = gain_terms.at[2 * norm_rows].set(grad_gain_q)
    gain_terms = gain_terms.at[2 * norm_rows + 1].set(grad_gain_k)
    grad_tokens, attn_weight_grad, sums_all = last_step(
        attn_input_part, inputs_own, grad_resid_own, gain_attn, gain_terms, attn_weight_part
    )

    def own_part(flat, like):
        return lax.dynamic_slice_in_dim(flat, b * like.shape[0], like.shape[0], 0)

    pieces = [0, q_cols, q_cols + k_cols, q_cols + 2 * k_cols, proj_cols, pack_attn.shape[1]]
    grads = [attn_weight_grad[:, lo:hi] for lo, hi in zip(pieces[:-1], pieces[1:])]
    return (
        output.reshape(tokens.shape),
        grad_tokens.astype(f32).reshape(tokens.shape),
        grads[0],
        grads[1],
        grads[2],
        grads[3],
        grads[4].T,
        mlp_weight_grad[:, :ff],
        mlp_weight_grad[:, ff : 2 * ff],
        mlp_weight_grad[:, 2 * ff :].T,
        own_part(sums_all[:norm_rows].reshape(-1), norm_attn),
        own_part(sums_all[norm_rows : 2 * norm_rows].reshape(-1), norm_mlp),
        own_part(sums_all[2 * norm_rows], gain_query),
        own_part(sums_all[2 * norm_rows + 1], gain_key),
    )


def solution(mesh):
    in_specs = (
        P(None, "batch", None),
        P(None, "batch", None),
        P(),
        P(),
        P(),
        P(),
        P("batch", "tensor"),
        P("batch", "tensor"),
        P("batch", "tensor"),
        P("batch", "tensor"),
        P("tensor", "batch"),
        P("batch", "tensor"),
        P("batch", "tensor"),
        P("tensor", "batch"),
        P("batch"),
        P("batch"),
        P("batch"),
        P("batch"),
    )
    out_specs = (
        P(None, "batch", None),
        P(None, "batch", None),
        P("batch", "tensor"),
        P("batch", "tensor"),
        P("batch", "tensor"),
        P("batch", "tensor"),
        P("tensor", "batch"),
        P("batch", "tensor"),
        P("batch", "tensor"),
        P("tensor", "batch"),
        P("batch"),
        P("batch"),
        P("batch"),
        P("batch"),
    )
    return jax.shard_map(shards, mesh=mesh, in_specs=in_specs, out_specs=out_specs, check_vma=False)
```

time: 1990 us -> 505 us (0.25)
  waiting for transfers between devices: 1260 us -> 0 us
  Pallas kernels: 0 us -> 390 us
  matrix products: 322 us -> 49.9 us
  blocking collectives: 176 us -> 0 us
  other arithmetic: 101 us -> 37.3 us
  local copies, waits for them, and re-layouts: 63.3 us -> 20.8 us
  loops' own time: 34.1 us -> 0 us
    reduce_scatter x7 -> x0, waiting for transfers between devices: 450 us -> none  [the longest x1 77 us: shards(): lax.psum_scatter(grad_gate.astype(jnp.bfloat16), 'batch', scatter_dimensi...]
    psum x3 -> x0, waiting for transfers between devices: 431 us -> none  [the longest x1 225 us: shards(): lax.psum(down_part.astype(jnp.bfloat16), 'tensor').astype(jnp.float32)]
    pallas_call x0 -> x8, Pallas kernels: none -> 390 us  [the longest x1 81.2 us: residual(): pl.pallas_call(residual_kernel, out_shape=[jax.ShapeDtypeStruct(part.shap...]
    dot_general x168 -> x15, matrix products: 322 us -> 49.9 us  [the longest x5 17.8 us: dot_t(): lax.dot_general(left, right, (((1,), (1,)), ((), ())), preferred_element_...]
    all_gather x8 -> x0, waiting for transfers between devices: 255 us -> none  [the longest x1 49.7 us: shards(): lax.all_gather(w_up, 'batch', axis=0, tiled=True)]
    unnamed x22 -> x0, waiting for transfers between devices: 120 us -> none
    all_gather x4 -> x0, blocking collectives: 91.6 us -> none  [the longest x1 24.2 us: shards(): lax.all_gather(norm_attn, 'batch', axis=0, tiled=True)]
    unnamed x2 -> x0, blocking collectives: 69.6 us -> none
  transfers between devices with their start and end apart: 20 -> 0, of which waited for: 19 -> 0; matrix products, arithmetic and copies ran while one was open for 9% -> 0% of each run, Pallas kernels for 0% -> 0%
where the time goes in v1:
time: 505 us; the launch traced here: 500 us
  Pallas kernels  390 us (77%)
  matrix products  49.9 us (10%)
  other arithmetic  37.3 us (7%)
  local copies, waits for them, and re-layouts  20.8 us (4%)
    pallas_call x1, Pallas kernels, residual(): pl.pallas_call(residual_kernel, out_shape=[jax.ShapeDtypeStruct(part.shap...  81.2 us
    pallas_call x1, Pallas kernels, output_and_kv(): pl.pallas_call(output_kernel, out_shape=[jax.ShapeDtypeStruct(part.shape,...  79.1 us
    pallas_call x1, Pallas kernels, mlp_back(): pl.pallas_call(mlp_back_kernel, out_shape=[jax.ShapeDtypeStruct(part.shap...  76.5 us
    pallas_call x1, Pallas kernels, last_step(): pl.pallas_call(last_kernel, out_shape=[jax.ShapeDtypeStruct(part.shape, b...  73.5 us
    pallas_call x2, Pallas kernels, batch_gather(): pl.pallas_call(functools.partial(batch_gather_kernel, count), out_shape=[...  60.1 us
    dot_general x5, matrix products, dot_t(): lax.dot_general(left, right, (((1,), (1,)), ((), ())), preferred_element_...  17.8 us
    dot_general x5, matrix products, t_dot(): lax.dot_general(left, right, (((0,), (0,)), ((), ())), preferred_element_...  16.2 us
    dot_general x5, matrix products, dot(): return jnp.dot(left, right, preferred_element_type=f32)  15.9 us

profile of v1, /device:TPU:1, one launch (start us, length us, event | category | flops | bytes accessed | tf_op | source)
XLA Modules:
  0.0 500.0 jit_solution(2465759611889625456)
XLA Ops:
  0.8 1.0 select_reduce_fusion
  3.7 2.3 multiply_reduce_fusion
  6.5 0.9 copy.148
  7.7 1.0 convert_multiply_fusion.grad_final
  8.7 1.0 dynamic-slice_convert_fusion.inputs
  9.7 2.1 multiply_cosine_fusion.1
  11.8 2.3 multiply_convert_fusion.1
  14.1 30.6 %attention_weights.1 = (bf16[16,128,1024]{2,1,0:T(8,128)(2,1)S(1)}, bf16[16,16,128]{2,1,0:T(8,128)(2,1)S(1)}) custom-call(bf16[128,1024]{1,0:T(8,128)(2,1)S(1)} %bitcast_dynamic-update-slice_fusion.refs_0_, bf16[16,128]{1,0:T(8,128)(2,1)S(1)} %scatter.29.refs_1_), custom_call_target="tpu_custom_call" | custom-call | tf_op jit(solution)/shard_map/attention_weights/pallas_call | solution.py:275
  44.7 2.1 copy-done.7
  47.0 4.9 fusion.1
  52.4 1.5 fusion.29
  54.1 0.9 fusion.50
  55.0 1.6 reshape.550
  58.6 29.5 %keys_and_values.1.kv_ref = bf16[16,640,256]{2,1,0:T(8,128)(2,1)S(1)} custom-call(bf16[640,256]{1,0:T(8,128)(2,1)S(1)} %pad_maximum_fusion.4.refs_0_), custom_call_target="tpu_custom_call" | custom-call | tf_op jit(solution)/shard_map/keys_and_values/pallas_call | solution.py:275
  88.2 11.6 %attention_forward.1 = (f32[2,640,128]{2,1,0:T(8,128)S(1)}, f32[2,640,128]{2,1,0:T(8,128)S(1)}) custom-call(bf16[2,640,128]{2,1,0:T(8,128)(2,1)S(1)} %bitcast.134, bf16[16,640,256]{2,1,0:T(8,128)(2,1)S(1)} %keys_and_values.1.kv_ref), custom_call_target="tpu_custom_call" | custom-call | tf_op jit(solution)/shard_map/attention_forward/pallas_call | solution.py:328
  100.6 1.3 fusion.14
  101.9 2.1 convolution_convert_fusion.6.part
  104.0 81.2 %residual_and_weights.1 = (bf16[640,2048]{1,0:T(8,128)(2,1)S(1)}, f32[80,2048]{1,0:T(8,128)S(1)}, bf16[16,128,768]{2,1,0:T(8,128)(2,1)S(1)}, bf16[16,128,768]{2,1,0:T(8,128)(2,1)S(1)}, bf16[16,128,768]{2,1,0:T(8,128)(2,1)}) custom-call(bf16[640,2048]{1,0:T(8,128)(2,1)S(1)} %convolution_convert_fusion.6.part, ...), custom_call_target="tpu_custom_call" | custom-call | tf_op jit(solution)/shard_map/residual_and_weights/pallas_call | solution.py:457
  185.3 2.2 fusion.54
  187.5 2.2 fusion.53
  190.2 2.8 multiply_convert_fusion.4
  193.0 3.7 convolution_convert_fusion.5.part
  196.7 2.2 fusion.55
  198.9 3.8 add_convert_fusion.part
  202.7 3.3 convolution_convert_fusion.2
  206.0 3.0 convolution_convert_fusion.3
  209.0 3.1 convolution_convert_fusion.1
  212.1 5.1 %pad_maximum_fusion.weight_part = bf16[2048,2304]{1,0:T(8,128)(2,1)} fusion(bf16[2048,768]{1,0:T(8,128)(2,1)S(1)} %convolution_convert_fusion.1, bf16[2048,768]{1,0:T(8,128)(2,1)S(1)} %convolution_convert_fusion.2, bf16[2048,768]{1,0:T(8,128)(2,1)S(1)} %convolution_convert_fusion.3), kind=kLoop, calls=%fused_computation | loop fusion | flops 28311552 | bytes 18874368 | tf_op jit(solution)/shard_map/concatenate | solution.py:844
  217.2 76.5 %mlp_grad_and_weights.1 = (bf16[640,2048]{1,0:T(8,128)(2,1)}, f32[80,2048]{1,0:T(8,128)}, f32[1,2048]{1,0:T(1,128)}, f32[128,2304]{1,0:T(8,128)}) custom-call(bf16[640,2048]{1,0:T(8,128)(2,1)} %add_convert_fusion.part, f32[80,2048]{1,0:T(8,128)} %copy-done.1, f32[80,2048]{1,0:T(8,128)} %convert_multiply_fusion.grad_final, f32[1,2048]{1,0:T(1,128)} %copy-done.10, ...), custom_call_target="tpu_custom_call" | custom-call | tf_op jit(solution)/shard_map/mlp_grad_and_weights/pallas_call | solution.py:526
  293.7 3.8 fusion.13
  297.5 2.0 convolution_convert_fusion.7
  300.2 8.3 %attention_backward.1 = (f32[2,640,128]{2,1,0:T(8,128)S(1)}, bf16[16,640,256]{2,1,0:T(8,128)(2,1)}) custom-call(bf16[2,640,128]{2,1,0:T(8,128)(2,1)S(1)} %bitcast.135, bf16[2,128,640]{2,1,0:T(8,128)(2,1)S(1)} %bitcast.139, bf16[2,640,128]{2,1,0:T(8,128)(2,1)S(1)} %bitcast.132, bf16[2,128,640]{2,1,0:T(8,128)(2,1)S(1)} %bitcast.140, ...), custom_call_target="tpu_custom_call" | custom-call | tf_op jit(solution)/shard_map/attention_backward/pallas_call | solution.py:390
  308.5 79.1 %output_and_kv_grads.1 = (bf16[640,2048]{1,0:T(8,128)(2,1)S(1)}, f32[640,256]{1,0:T(8,128)S(1)}) custom-call(bf16[640,2048]{1,0:T(8,128)(2,1)} %convolution_convert_fusion.5.part, f32[80,2048]{1,0:T(8,128)S(1)} %copy-done.2, bf16[16,640,256]{2,1,0:T(8,128)(2,1)} %get-tuple-element.128.kv_part), custom_call_target="tpu_custom_call" | custom-call | tf_op jit(solution)/shard_map/output_and_kv_grads/pallas_call | solution.py:577
  388.0 1.0 copy-done.12
  389.7 2.8 copy_bitcast_fusion
  392.6 1.0 slice.298
  393.6 1.5 fusion.32
  395.1 1.6 fusion.36
  396.8 1.5 fusion.38
  398.3 5.9 %convolution_convert_fusion.4.part = bf16[640,2048]{1,0:T(8,128)(2,1)} fusion(bf16[2048,1024]{1,0:T(8,128)(2,1)} %bitcast.146, bf16[640,256]{1,0:T(8,128)(2,1)} %get-tuple-element.231, bf16[640,128]{1,0:T(8,128)(2,1)S(1)} %slice.298, bf16[640,128]{1,0:T(8,128)(2,1)S(1)} %fusion.38, bf16[640,256]{1,0:T(8,128)(2,1)} %copy_bitcast_fusion), kind=kOutput, calls=%fused_computation.11 | convolution fusion | flops 2018508800 | bytes 6750208 | tf_op jit(solution)/shard_map/dot_general | solution.py:715
  404.2 1.0 slice_bitcast_fusion
  405.3 1.9 copy.170
  407.2 4.8 convolution_convert_fusion
  412.0 2.6 pad_maximum_fusion.1.weight_part
  414.6 73.5 %input_grad_and_weights.1 = (bf16[640,2048]{1,0:T(8,128)(2,1)S(1)}, f32[128,1024]{1,0:T(8,128)S(1)}, f32[40,128]{1,0:T(8,128)S(1)}) custom-call(bf16[640,2048]{1,0:T(8,128)(2,1)} %convolution_convert_fusion.4.part, f32[80,2048]{1,0:T(8,128)S(1)} %dynamic-slice_convert_fusion.inputs, f32[80,2048]{1,0:T(8,128)S(1)} %copy-done.4, ...), custom_call_target="tpu_custom_call" | custom-call | tf_op jit(solution)/shard_map/input_grad_and_weights/pallas_call | solution.py:657
  488.2 1.5 copy-done.3
  493.6 4.8 convert.31
  498.4 1.5 copy.200
  (144 shorter events, 12.2 us)
Async XLA Ops:
  0.6 7.1 %copy-start.17 = (bf16[2,320,2048]{2,1,0:T(8,128)(2,1)S(1)}, bf16[2,320,2048]{2,1,0:T(8,128)(2,1)}, u32[]{:S(2)}) copy-start(bf16[2,320,2048]{2,1,0:T(8,128)(2,1)} %param.33) | copy-start | bytes 7864324
  0.7 5.7 %copy-start.38 = (bf16[8]{0:T(256)(128)(2,1)S(1)}, bf16[8]{0:T(256)(128)(2,1)}, u32[]{:S(2)}) copy-start(bf16[8]{0:T(256)(128)(2,1)} %param.49) | copy-start | bytes 52
  0.7 5.5 %copy-start.37 = (bf16[8]{0:T(256)(128)(2,1)S(1)}, bf16[8]{0:T(256)(128)(2,1)}, u32[]{:S(2)}) copy-start(bf16[8]{0:T(256)(128)(2,1)} %param.48) | copy-start | bytes 52
  0.7 5.4 %copy-start.36 = (bf16[128]{0:T(256)(128)(2,1)S(1)}, bf16[128]{0:T(256)(128)(2,1)}, u32[]{:S(2)}) copy-start(bf16[128]{0:T(256)(128)(2,1)} %param.47) | copy-start | bytes 772
  0.7 5.4 %copy-start.35 = (bf16[128]{0:T(256)(128)(2,1)S(1)}, bf16[128]{0:T(256)(128)(2,1)}, u32[]{:S(2)}) copy-start(bf16[128]{0:T(256)(128)(2,1)} %param.46) | copy-start | bytes 772
  0.7 6.7 %copy-start.28 = (bf16[768,128]{1,0:T(8,128)(2,1)S(1)}, bf16[768,128]{1,0:T(8,128)(2,1)}, u32[]{:S(2)}) copy-start(bf16[768,128]{1,0:T(8,128)(2,1)} %param.45) | copy-start | bytes 589828
  0.7 7.0 %copy-start.31 = (bf16[128,256]{1,0:T(8,128)(2,1)S(1)}, bf16[128,256]{1,0:T(8,128)(2,1)}, u32[]{:S(2)}) copy-start(bf16[128,256]{1,0:T(8,128)(2,1)} %param.41) | copy-start | bytes 196612
  0.7 6.9 %copy-start.33 = (bf16[128,128]{1,0:T(8,128)(2,1)S(1)}, bf16[128,128]{1,0:T(8,128)(2,1)}, u32[]{:S(2)}) copy-start(bf16[128,128]{1,0:T(8,128)(2,1)} %param.40) | copy-start | bytes 98308
  0.7 6.9 %copy-start.32 = (bf16[128,128]{1,0:T(8,128)(2,1)S(1)}, bf16[128,128]{1,0:T(8,128)(2,1)}, u32[]{:S(2)}) copy-start(bf16[128,128]{1,0:T(8,128)(2,1)} %param.39) | copy-start | bytes 98308
  0.7 6.9 %copy-start.30 = (bf16[128,256]{1,0:T(8,128)(2,1)S(1)}, bf16[128,256]{1,0:T(8,128)(2,1)}, u32[]{:S(2)}) copy-start(bf16[128,256]{1,0:T(8,128)(2,1)} %param.38) | copy-start | bytes 196612
  44.7 2.1 copy-start.7
  46.8 57.2 %copy-start.10 = (f32[1,2048]{1,0:T(1,128)}, f32[1,2048]{1,0:T(1,128)S(1)}, u32[]{:S(2)}) copy-start(f32[1,2048]{1,0:T(1,128)S(1)} %get-tuple-element.252.gain) | copy-start | bytes 24580
  52.0 3.0 copy-start.15
  54.1 3.8 copy-start.19
  54.1 3.8 copy-start.21
  55.0 3.2 copy-start.11
  88.2 11.6 %copy-start = (bf16[16,640,256]{2,1,0:T(8,128)(2,1)}, bf16[16,640,256]{2,1,0:T(8,128)(2,1)S(1)}, u32[]{:S(2)}) copy-start(bf16[16,640,256]{2,1,0:T(8,128)(2,1)S(1)} %keys_and_values.1.kv_ref) | copy-start | bytes 15728644
  100.5 3.5 copy-start.8
  100.6 3.5 copy-start.9
  185.3 2.2 copy-start.1
  187.5 2.2 copy-start.25
  187.5 2.7 copy-start.39
  206.0 3.0 copy-start.18
  217.2 76.5 %copy-start.16 = (f32[640,768]{1,0:T(8,128)S(1)}, f32[640,768]{1,0:T(8,128)}, u32[]{:S(2)}) copy-start(f32[640,768]{1,0:T(8,128)} %copy-done.15) | copy-start | bytes 5898244
  293.7 3.8 copy-start.40
  297.5 2.5 copy-start.34
  300.2 8.3 %copy-start.2 = (f32[80,2048]{1,0:T(8,128)S(1)}, f32[80,2048]{1,0:T(8,128)}, u32[]{:S(2)}) copy-start(f32[80,2048]{1,0:T(8,128)} %copy-done.1) | copy-start | bytes 1966084
  308.5 79.2 %copy-start.20 = (f32[640,64]{1,0:T(8,128)S(1)}, f32[640,64]{1,0:T(8,128)}, u32[]{:S(2)}) copy-start(f32[640,64]{1,0:T(8,128)} %get-tuple-element.258) | copy-start | bytes 491524
  308.5 79.2 %copy-start.22 = (f32[640,64]{1,0:T(8,128)S(1)}, f32[640,64]{1,0:T(8,128)}, u32[]{:S(2)}) copy-start(f32[640,64]{1,0:T(8,128)} %get-tuple-element.259) | copy-start | bytes 491524
  387.6 2.0 copy-start.5
  387.6 1.4 copy-start.12
  388.0 1.6 copy-start.13
  388.0 1.6 copy-start.14
  389.7 3.9 copy-start.6
  395.1 1.6 copy-start.23
  395.1 1.6 copy-start.24
  398.3 5.9 %copy-start.29 = (bf16[640,128]{1,0:T(8,128)(2,1)}, bf16[640,128]{1,0:T(8,128)(2,1)S(1)}, u32[]{:S(2)}) copy-start(bf16[640,128]{1,0:T(8,128)(2,1)S(1)} %fusion.38) | copy-start | bytes 491524
  398.3 5.9 %copy-start.26 = (f32[128,2304]{1,0:T(8,128)S(1)}, f32[128,2304]{1,0:T(8,128)}, u32[]{:S(2)}) copy-start(f32[128,2304]{1,0:T(8,128)} %get-tuple-element.136) | copy-start | bytes 3538948
  407.2 4.8 copy-start.27
  412.0 2.6 copy-start.4
  488.2 1.5 copy-start.3

commit v2 on v1

--- a/solution.py
+++ b/solution.py
@@ -1,4 +1,5 @@
 import functools
+import itertools
 import math
 
 import jax
@@ -19,35 +20,37 @@
 
 
 class Group:
-    def __init__(self, kind):
+    def __init__(self, kind, core=True):
         b = lax.axis_index("batch")
         t = lax.axis_index("tensor")
+        c = lax.rem(b, 2)
+        self.c, self.t = c, t
         if kind == "tensor":
             r, q = lax.div(t, 2), lax.rem(t, 2)
             self.slot = lambda dr, dq: lax.rem(r + dr, 4) * 2 + lax.rem(q + dq, 2)
             at = lambda dr, dq: (b, self.slot(dr, dq))
-            self.core = None
         else:
-            c = lax.rem(b, 2)
             q, r = lax.div(b, 8), lax.rem(lax.div(b, 2), 4)
-            self.slot = lambda dr, dq, dc=0: (
-                lax.rem(q + dq, 2) * 4 + lax.rem(r + dr, 4)
-            ) * 2 + lax.rem(c + dc, 2)
+            self.chip = lambda dr, dq: lax.rem(q + dq, 2) * 4 + lax.rem(r + dr, 4)
+            self.slot = lambda dr, dq, dc=0: self.chip(dr, dq) * 2 + lax.rem(c + dc, 2)
             at = lambda dr, dq: (self.slot(dr, dq), t)
-            self.core = (self.slot(0, 0, 1), t)
+        self.core = (b + 1 - 2 * c, t) if core else None
         self.right, self.left, self.mate = at(1, 0), at(3, 0), at(0, 1)
-
-    def neighbours(self):
-        near = [self.right, self.left, self.mate]
-        return near + ([self.core] if self.core is not None else [])
-
-
-def enter(groups):
+        self.others = [at(dr, dq) for dr in range(4) for dq in range(2) if dr or dq]
+        self.steps = [(dr, dq) for dr in range(4) for dq in range(2) if dr or dq]
+
+
+def enter(devices):
     barrier = pltpu.get_barrier_semaphore()
-    near = [device for group in groups for device in group.neighbours()]
-    for device in near:
+    for device in devices:
         pl.semaphore_signal(barrier, inc=1, device_id=device, device_id_type=MESH)
-    pl.semaphore_wait(barrier, len(near))
+    pl.semaphore_wait(barrier, len(devices))
+
+
+def near(*groups):
+    devices = [d for g in groups for d in (g.right, g.left, g.mate)]
+    cores = [g.core for g in groups if g.core is not None]
+    return devices + cores[:1]
 
 
 class Copies:
@@ -78,7 +81,8 @@
 
 def half_of(ref, which):
     width = ref.shape[-1] // 2
-    return ref.at[:, pl.ds(which * width, width)]
+    lead = (slice(None),) * (len(ref.shape) - 1)
+    return ref.at[lead + (pl.ds(which * width, width),)]
 
 
 def run_all(*steps):
@@ -91,7 +95,7 @@
                 waiting.remove(step)
 
 
-def gather(copies, group, own, slot, split=True):
+def gather(copies, group, own, slot, split=True, source=None):
     s = group.slot
     core_copies = []
     sent = []
@@ -105,15 +109,23 @@
         if group.core is not None:
             core_copies.extend(push(ref, group.core))
 
+    def core_wait(count):
+        for copy in core_copies[:count]:
+            copy.wait_recv()
+        del core_copies[:count]
+
     home = slot(s(0, 0))
-    first = [copies.send(own, home, d) for d in (group.right, group.left, group.mate)]
+    source = own if source is None else source
+    first = [copies.send(source, home, d) for d in (group.right, group.left, group.mate)]
     sent.extend(first)
-    if group.core is not None:
-        core_copies.append(copies.send(own, home, group.core))
-        sent.append(core_copies[0])
-    kept = copies.local(own, home)
+    kept = None
+    if own is not None:
+        kept = copies.local(own, home)
+        if group.core is not None:
+            core_copies.append(copies.send(own, home, group.core))
+            sent.append(core_copies[0])
     from_left, from_right, from_mate = first
-    yield
+    yield []
     from_left.wait_recv()
     left_unit = slot(s(3, 0))
     far = push(half_of(left_unit, 0) if split else left_unit, group.right)
@@ -127,30 +139,30 @@
     mate_unit = slot(s(0, 1))
     mate_left, mate_right = push(mate_unit, group.right, group.left)
     to_core(mate_unit)
-    yield
-    mate_left.wait_recv()
-    left_unit = slot(s(3, 1))
-    mate_far = push(half_of(left_unit, 0) if split else left_unit, group.right)
-    to_core(left_unit)
-    mate_right.wait_recv()
-    right_unit = slot(s(1, 1))
-    if split:
-        mate_far += push(half_of(right_unit, 1), group.left)
-    to_core(right_unit)
-    yield
+    if own is not None:
+        core_wait(1)
+        kept.wait()
+    yield [(0, 0)]
     for copy in far:
         copy.wait_recv()
-    to_core(slot(s(2, 0)))
-    yield
-    for copy in mate_far:
-        copy.wait_recv()
+    far_unit = slot(s(2, 0))
+    (mate_far,) = push(far_unit, group.mate)
+    to_core(far_unit)
+    yield []
+    mate_left.wait_recv()
+    to_core(slot(s(3, 1)))
+    mate_right.wait_recv()
+    to_core(slot(s(1, 1)))
+    core_wait(3)
+    yield [(3, 0), (1, 0), (0, 1)]
+    mate_far.wait_recv()
     to_core(slot(s(2, 1)))
-    yield
-    for copy in core_copies:
-        copy.wait_recv()
+    core_wait(3)
+    yield [(2, 0), (3, 1), (1, 1)]
+    core_wait(1)
+    yield [(2, 1)]
     for copy in sent:
         copy.wait_send()
-    kept.wait()
 
 
 def add_rows(target, sources, step=16):
@@ -257,83 +269,314 @@
     )
 
 
-def batch_gather_kernel(count, *refs):
-    own, out = refs[:count], refs[count : 2 * count]
-    copies = Copies(*refs[2 * count :])
-    group = Group("batch")
-    enter([group])
-    run_all(
-        *[
-            gather(copies, group, own[n], functools.partial(lambda o, s: o.at[s], out[n]), n == 0)
-            for n in range(count)
-        ]
-    )
-
-
-def batch_gather(name, collective, *arrays):
-    count = len(arrays)
-    return pl.pallas_call(
-        functools.partial(batch_gather_kernel, count),
-        out_shape=[jax.ShapeDtypeStruct((16,) + a.shape, a.dtype) for a in arrays],
-        in_specs=[ANY] * count,
-        out_specs=[ANY] * count,
-        scratch_shapes=sems(24 * count, count),
-        name=name,
-        compiler_params=params(collective, 16),
-    )(*arrays)
-
-
-def forward_kernel(scale, q_ref, kv_ref, out_ref, sum_ref, acc_ref):
+def rows_at(i, step=16):
+    return pl.ds(pl.multiple_of(i * step, step), step)
+
+
+def each_rows(rows, step, body):
+    def run(i, carry):
+        body(rows_at(i, step))
+        return carry
+
+    lax.fori_loop(0, rows // step, run, 0)
+
+
+def prepare_head(values, gain, cosine, sine):
+    half_size = values.shape[1] // 2
+    mean = jnp.mean(values * values, axis=-1, keepdims=True)
+    scaled = values * lax.rsqrt(mean + epsilon) * gain
+    return scaled * cosine + pltpu.roll(scaled, half_size, 1) * sine
+
+
+def forward_kernel(
+    scale,
+    tokens,
+    cosine,
+    sine,
+    pack_a,
+    pack_b,
+    mlp_a,
+    mlp_b,
+    mlp_c,
+    normed_out,
+    query_raw,
+    kv_raw,
+    gate_raw,
+    queries,
+    kv_out,
+    attended,
+    lse,
+    gated,
+    normed_mlp,
+    resid,
+    wide_kvo,
+    wide_qg,
+    w_out_out,
+    wide_a,
+    wide_b,
+    wide_c,
+    gain_wide,
+    gain_head,
+    normed,
+    inverse,
+    w_kvo,
+    w_qg,
+    w_out,
+    kv_own,
+    kv_all,
+    acc,
+    rows_all,
+    own,
+    send_sem,
+    recv_sem,
+    local_sem,
+):
+    copies = Copies(send_sem, recv_sem, local_sem)
+    tensor, batch = Group("tensor"), Group("batch")
     b = lax.axis_index("batch")
-    seqs, rows, head = q_ref.shape
-    seq_dev = kv_ref.shape[1] // seqs
+    rows, width = tokens.shape
+    cols = query_raw.shape[1]
+    own_rows = resid.shape[0]
+    seqs, head_rows, head = queries.shape
+    heads = query_raw.shape[1] // head
+    seq_dev = rows // seqs
+    enter(tensor.others + near(batch))
+
+    def batch_gather(source, target, split=True):
+        return gather(copies, batch, source, lambda s: target.at[s], split)
+
+    a_steps = batch_gather(pack_a, w_kvo)
+    b_steps = batch_gather(pack_b, w_qg)
+    next(a_steps)
+    next(b_steps)
+
+    def invert(at):
+        values = tokens[at, :].astype(f32)
+        mean = jnp.mean(values * values, axis=-1, keepdims=True)
+        inverse[at, :] = jnp.broadcast_to(lax.rsqrt(mean + epsilon), (16, 128))
+
+    each_rows(rows, 16, invert)
+    next(a_steps)
+    next(b_steps)
+    for _ in a_steps:
+        pass
+    depth = pack_b.shape[0]
+    half = tensor.c * 8
+    kept = [copies.local(w_kvo, wide_kvo)]
+    out_home = copies.local(w_kvo.at[:, pl.ds(0, depth), pl.ds(cols, cols)], w_out.at[tensor.t])
+    wide_out_steps = gather(
+        copies,
+        tensor,
+        None,
+        lambda s: w_out.at[s, pl.ds(half, 8)],
+        source=w_kvo.at[pl.ds(half, 8), pl.ds(0, depth), pl.ds(cols, cols)],
+    )
+    next(wide_out_steps)
+    gain_wide[...] = jnp.zeros_like(gain_wide)
+    gain_head[...] = jnp.zeros_like(gain_head)
+    total = jnp.zeros((16, 128), f32)
+    for n in range(16):
+        entry = w_kvo[n, depth:, 0:128].astype(f32)
+        gain_wide[0:2, n * 128 : (n + 1) * 128] = entry[0:2]
+        total = total + entry
+    gain_head[0:2, :] = total[2:4]
+
+    def normalise(at):
+        scaled = tokens[at, :].astype(f32) * inverse[at, 0:1] * gain_wide[0:1, :]
+        normed[at, :] = scaled.astype(bf16)
+
+    each_rows(rows, 16, normalise)
+    kept.append(copies.local(normed, normed_out))
+
+    def project(weights, at):
+        return jnp.dot(normed[at, :], weights.reshape(width, cols), preferred_element_type=f32)
+
+    for s in range(seqs):
+        at = pl.ds(s * seq_dev, seq_dev)
+        raw = project(w_kvo[:, 0:depth, 0:cols], at)
+        kv_raw[at, :] = raw
+        key = prepare_head(raw[:, :head], gain_head[1:2, :], cosine[...], sine[...])
+        kv_own[at, :head] = key.astype(bf16)
+        kv_own[at, head:] = raw[:, head:].astype(bf16)
+    all_steps = batch_gather(kv_own, kv_all)
+    next(all_steps)
+    for _ in b_steps:
+        pass
+    kept.append(copies.local(w_qg, wide_qg))
+    for s in range(seqs):
+        at = pl.ds(s * seq_dev, seq_dev)
+        raw = project(w_qg[:, :, 0:cols], at)
+        query_raw[at, :] = raw
+        for h in range(heads):
+            values = prepare_head(
+                raw[:, h * head : (h + 1) * head], gain_head[0:1, :], cosine[...], sine[...]
+            )
+            queries[s, h * seq_dev : (h + 1) * seq_dev, :] = values.astype(bf16)
+        gate_raw[at, :] = project(w_qg[:, :, cols:], at)
+
     factor = scale * math.log2(math.e)
     ones = jnp.ones((2 * seq_dev, head), bf16)
-    last = lax.div(b, 2)
-    tile = rows // 4
-    for s in range(seqs):
-        at = pl.ds(s * seq_dev, seq_dev)
-
-        def block(pair, masked):
-            first, second = pair * 2, pair * 2 + 1
-            keys = jnp.concatenate([kv_ref[first, at, :head], kv_ref[second, at, :head]], axis=0)
-            values = jnp.concatenate([kv_ref[first, at, head:], kv_ref[second, at, head:]], axis=0)
+    tile = head_rows // 4
+    acc[...] = jnp.zeros_like(acc)
+
+    def block(pair, masked):
+        def body(s, carry):
+            at = rows_at(s, seq_dev)
+            keys = jnp.concatenate(
+                [kv_all[pair * 2, at, :head], kv_all[pair * 2 + 1, at, :head]], axis=0
+            )
+            values = jnp.concatenate(
+                [kv_all[pair * 2, at, head:], kv_all[pair * 2 + 1, at, head:]], axis=0
+            )
             wide = jnp.concatenate([values, ones], axis=1)
             for i in range(4):
                 here = pl.ds(i * tile, tile)
                 scores = lax.dot_general(
-                    q_ref[s, here, :], keys, (((1,), (1,)), ((), ())), preferred_element_type=f32
+                    queries[s, here, :], keys, (((1,), (1,)), ((), ())), preferred_element_type=f32
                 )
                 weights = jnp.exp2(scores * factor)
                 if masked:
                     row = lax.broadcasted_iota(jnp.int32, scores.shape, 0) + (i * tile) % seq_dev
                     col = lax.broadcasted_iota(jnp.int32, scores.shape, 1)
-                    weights = jnp.where(col + first * seq_dev <= row + b * seq_dev, weights, 0.0)
-                acc_ref[here, :] += jnp.dot(weights.astype(bf16), wide, preferred_element_type=f32)
-
-        acc_ref[...] = jnp.zeros_like(acc_ref)
-
-        def body(pair, carry):
-            block(pair, False)
+                    ahead = (pair * 2 - b) * seq_dev
+                    weights = jnp.where(col + ahead <= row, weights, 0.0)
+                acc[s, here, :] += jnp.dot(weights.astype(bf16), wide, preferred_element_type=f32)
             return carry
 
-        lax.fori_loop(0, last, body, 0)
-        block(last, True)
-        out_ref[s] = acc_ref[:, :head] / acc_ref[:, head:]
-        sum_ref[s] = acc_ref[:, head:]
-
-
-def attention_forward(queries, kv_all, scale):
-    shape = jax.ShapeDtypeStruct(queries.shape, f32)
+        lax.fori_loop(0, seqs, body, 0)
+
+    here = batch.chip(0, 0)
+
+    def attend(ready):
+        for dr, dq in ready:
+            if (dr, dq) == (0, 0):
+                block(here, True)
+            else:
+                pair = batch.chip(dr, dq)
+
+                @pl.when(pair < here)
+                def _():
+                    block(pair, False)
+
+    mlp_steps = [
+        batch_gather(mlp_a, wide_a),
+        batch_gather(mlp_b, wide_b),
+        batch_gather(mlp_c, wide_c),
+    ]
+    attend(next(all_steps))
+    next(wide_out_steps)
+    attend(next(all_steps))
+    next(wide_out_steps)
+    ready = next(all_steps)
+    for step in mlp_steps:
+        next(step)
+    attend(ready)
+    ready = next(all_steps)
+    next(wide_out_steps)
+    attend(ready)
+    attend(next(all_steps))
+    for _ in all_steps:
+        pass
+    kept.append(copies.local(kv_all, kv_out))
+    for s in range(seqs):
+        sums = acc[s, :, head:]
+        lse[s] = jnp.log2(sums).T[0:1, :]
+        out = acc[s, :, :head] / sums
+        for h in range(heads):
+            at, cols = pl.ds(s * seq_dev, seq_dev), pl.ds(h * head, head)
+            part = out[h * seq_dev : (h + 1) * seq_dev]
+            attended[at, cols] = part
+            gated[at, cols] = (part * jax.nn.sigmoid(gate_raw[at, cols])).astype(bf16)
+
+    def unit_rows(ref, slot):
+        return ref.at[pl.ds(pl.multiple_of(slot * own_rows, 16), own_rows), :]
+
+    exchanged = [
+        copies.send(unit_rows(gated, tensor.slot(*step)), rows_all.at[tensor.t], device)
+        for step, device in zip(tensor.steps, tensor.others)
+    ]
+    rows_all[tensor.t] = unit_rows(gated, tensor.t)[...]
+    run_all(wide_out_steps, *[itertools.islice(step, 1) for step in mlp_steps])
+    out_home.wait()
+    kept.append(copies.local(w_out, w_out_out))
+    for copy in exchanged:
+        copy.wait_recv()
+    resid[...] = unit_rows(tokens, tensor.t)[...].astype(f32)
+
+    def out_term(n, carry):
+        resid[...] += lax.dot_general(
+            rows_all[n],
+            w_out[n].reshape(width, -1),
+            (((1,), (1,)), ((), ())),
+            preferred_element_type=f32,
+        )
+        return carry
+
+    lax.fori_loop(0, 8, out_term, 0)
+
+    def normalise_own(at):
+        values = resid[at, :]
+        mean = jnp.mean(values * values, axis=-1, keepdims=True)
+        own[at, :] = (values * lax.rsqrt(mean + epsilon) * gain_wide[1:2, :]).astype(bf16)
+
+    each_rows(own_rows, 16, normalise_own)
+    tensor.core = None
+    own_steps = gather(copies, tensor, own, lambda s: unit_rows(normed_mlp, s))
+    run_all(own_steps, *mlp_steps)
+    for copy in exchanged:
+        copy.wait_send()
+    for copy in kept:
+        copy.wait()
+
+
+def forward(tokens, cosine, sine, packs, mlp_packs, scale, seqs):
+    rows, width = tokens.shape
+    cols = packs[1].shape[1] // 2
+    head = cosine.shape[1]
+    own_rows = rows // 8
+    heads = cols // head
+    shape = jax.ShapeDtypeStruct
+    weight_a, weight_b = (16,) + packs[0].shape, (16,) + packs[1].shape
+    weight_out = (8, 16, packs[1].shape[0], cols)
+    outs = [
+        (shape((rows, width), bf16), ANY),
+        (shape((rows, cols), f32), VM),
+        (shape((rows, cols), f32), VM),
+        (shape((rows, cols), f32), VM),
+        (shape((seqs, heads * rows // seqs, head), bf16), VM),
+        (shape((16, rows, cols), bf16), ANY),
+        (shape((rows, cols), f32), VM),
+        (shape((seqs, 1, heads * rows // seqs), f32), VM),
+        (shape((rows, cols), bf16), VM),
+        (shape((rows, width), bf16), ANY),
+        (shape((own_rows, width), f32), VM),
+        (shape(weight_a, bf16), ANY),
+        (shape(weight_b, bf16), ANY),
+        (shape(weight_out, bf16), ANY),
+    ]
+    outs += [(shape((16,) + p.shape, bf16), ANY) for p in mlp_packs]
+    outs += [(shape((8, width), f32), VM), (shape((8, head), f32), VM)]
     return pl.pallas_call(
         functools.partial(forward_kernel, scale),
-        out_shape=[shape, shape],
-        in_specs=[VM, VM],
-        out_specs=[VM, VM],
-        scratch_shapes=[pltpu.VMEM((queries.shape[1], 2 * queries.shape[2]), f32)],
-        name="attention_forward",
-        compiler_params=pltpu.CompilerParams(vmem_limit_bytes=40 * MIB),
-    )(queries, kv_all)
+        out_shape=[o for o, _ in outs],
+        in_specs=[VM] * 3 + [ANY] * 5,
+        out_specs=[s for _, s in outs],
+        scratch_shapes=[
+            pltpu.VMEM((rows, width), bf16),
+            pltpu.VMEM((rows, 128), f32),
+            pltpu.VMEM(weight_a, bf16),
+            pltpu.VMEM(weight_b, bf16),
+            pltpu.VMEM(weight_out, bf16),
+            pltpu.VMEM((rows, cols), bf16),
+            pltpu.VMEM((16, rows, cols), bf16),
+            pltpu.VMEM((seqs, heads * rows // seqs, 2 * head), f32),
+            pltpu.VMEM((8, own_rows, cols), bf16),
+            pltpu.VMEM((own_rows, width), bf16),
+        ]
+        + sems(24 * 12, 24),
+        name="forward",
+        compiler_params=params(1, 56),
+    )(tokens, cosine, sine, *packs, *mlp_packs)
 
 
 def backward_kernel(
@@ -409,68 +652,6 @@
     )
 
 
-def rows_at(i, step=16):
-    return pl.ds(pl.multiple_of(i * step, step), step)
-
-
-def residual_kernel(
-    part, inputs, gain, pack_a, pack_b, pack_c, normed, resid, wide_a, wide_b, wide_c, *rest
-):
-    scratch, own, (send_sem, recv_sem, local_sem) = rest[:4], rest[4], rest[5:]
-    copies = Copies(send_sem, recv_sem, local_sem)
-    tensor, batch = Group("tensor"), Group("batch")
-    rows = resid.shape[0]
-    enter([tensor, batch])
-
-    def along():
-        def unit(dr, dq):
-            return part.at[pl.ds(pl.multiple_of(tensor.slot(dr, dq) * rows, 16), rows), :]
-
-        yield from reduce(copies, tensor, unit, scratch, resid)
-
-        def body(i, carry):
-            at = rows_at(i)
-            total = inputs[at, :] + resid[at, :]
-            resid[at, :] = total
-            mean = jnp.mean(total * total, axis=-1, keepdims=True)
-            own[at, :] = (total * lax.rsqrt(mean + epsilon) * gain[...]).astype(bf16)
-            return carry
-
-        lax.fori_loop(0, rows // 16, body, 0)
-        yield from gather(
-            copies,
-            tensor,
-            own,
-            lambda s: normed.at[pl.ds(pl.multiple_of(s * rows, 16), rows), :],
-        )
-
-    run_all(
-        gather(copies, batch, pack_a, lambda s: wide_a.at[s]),
-        gather(copies, batch, pack_b, lambda s: wide_b.at[s]),
-        gather(copies, batch, pack_c, lambda s: wide_c.at[s]),
-        along(),
-    )
-
-
-def residual(part, inputs, gain, packs):
-    rows, width = inputs.shape
-    return pl.pallas_call(
-        residual_kernel,
-        out_shape=[
-            jax.ShapeDtypeStruct(part.shape, bf16),
-            jax.ShapeDtypeStruct(inputs.shape, f32),
-        ]
-        + [jax.ShapeDtypeStruct((16,) + p.shape, bf16) for p in packs],
-        in_specs=[VM] * 3 + [ANY] * len(packs),
-        out_specs=[ANY, VM] + [ANY] * len(packs),
-        scratch_shapes=reduce_scratch(rows, width, False)
-        + [pltpu.VMEM((rows, width), bf16)]
-        + sems(24 * 5, 5),
-        name="residual_and_weights",
-        compiler_params=params(3, 40),
-    )(part, inputs, gain, *packs)
-
-
 def norm_back(values, gain, grad):
     inverse = lax.rsqrt(jnp.mean(values * values, axis=-1, keepdims=True) + epsilon)
     scaled = grad * gain
@@ -485,10 +666,10 @@
     scratch, scratch_w = rest[:4], rest[4:10]
     own, total = rest[10], rest[11]
     copies = Copies(*rest[12:])
-    tensor, batch = Group("tensor"), Group("batch")
+    tensor, batch = Group("tensor", False), Group("batch")
     rows = resid.shape[0]
     depth = weight_grad.shape[0]
-    enter([tensor, batch])
+    enter(near(tensor, batch))
 
     def along():
         def unit(dr, dq):
@@ -546,9 +727,9 @@
     scratch, scratch_kv = rest[:4], rest[4:10]
     own, final = rest[10], rest[11]
     copies = Copies(*rest[12:])
-    tensor, batch = Group("tensor"), Group("batch")
+    tensor, batch = Group("tensor", False), Group("batch")
     rows = resid.shape[0]
-    enter([tensor, batch])
+    enter(near(tensor, batch))
 
     def along():
         def unit(dr, dq):
@@ -597,10 +778,10 @@
     scratch, scratch_w = rest[:4], rest[4:10]
     own, held, total, mine, over_tensor, mine_too, over_batch = rest[10:17]
     copies = Copies(*rest[17:])
-    tensor, batch = Group("tensor"), Group("batch")
+    tensor, batch = Group("tensor", False), Group("batch")
     rows, width = inputs.shape
     depth = weight_grad.shape[0]
-    enter([tensor, batch])
+    enter(near(tensor, batch))
 
     def small():
         yield from gather(copies, tensor, mine, lambda s: over_tensor.at[s], False)
@@ -751,44 +932,74 @@
     q_cols, k_cols = w_query.shape[1], w_key.shape[1]
     heads = q_cols // head
 
-    pack_attn = jnp.concatenate([w_query, w_key, w_value, w_gate_out, w_output.T], axis=1)
-    few = jnp.zeros((16, norm_attn.shape[0]), bf16)
-    few = few.at[0].set(norm_attn).at[1].set(norm_mlp)
-    few = few.at[2, : gain_query.shape[0]].set(gain_query)
-    few = few.at[3, : gain_key.shape[0]].set(gain_key)
-    wide_attn, wide_few = batch_gather("attention_weights", 1, pack_attn, few)
-    wide_attn = wide_attn.reshape(width, pack_attn.shape[1])
-    proj_cols = 2 * q_cols + 2 * k_cols
-    w_proj = wide_attn[:, :proj_cols]
-    w_out_t = wide_attn[:, proj_cols:]
-    gain_attn = wide_few[:, 0].reshape(1, width).astype(f32)
-    gain_mlp = wide_few[:, 1].reshape(1, width).astype(f32)
-    gain_q = wide_few[:, 2, : gain_query.shape[0]].reshape(head).astype(f32)
-    gain_k = wide_few[:, 3, : gain_key.shape[0]].reshape(head).astype(f32)
+    gains = jnp.zeros((2, head), bf16)
+    gains = lax.dynamic_update_slice(
+        gains, jnp.stack([gain_query, gain_key]), (0, b * gain_query.shape[0])
+    )
+    few = jnp.concatenate(
+        [norm_attn[None], norm_mlp[None], gains, jnp.zeros((12, head), bf16)], axis=0
+    )
+    few = jnp.pad(few, ((0, 0), (0, 2 * k_cols + q_cols - head)))
+    packs = (
+        jnp.concatenate([jnp.concatenate([w_key, w_value, w_output.T], axis=1), few], axis=0),
+        jnp.concatenate([w_query, w_gate_out], axis=1),
+    )
 
     half_size = head // 2
-    pos_local = b * seq_dev + jnp.arange(seq_dev, dtype=jnp.int32)
+    pos_local = (b * seq_dev + jnp.arange(seq_dev, dtype=jnp.int32)).astype(f32)
     inverse_freq = rope_base ** (-jnp.arange(half_size, dtype=f32) / half_size)
-    row_pos = jnp.tile(pos_local, seq_count).astype(f32)
-    angles = row_pos[:, None] * inverse_freq[None, :]
-    cosine = jnp.cos(angles)[:, None, :]
-    sine = jnp.sin(angles)[:, None, :]
+    angles = pos_local[:, None] * inverse_freq[None, :]
+    cosine, sine = jnp.cos(angles), jnp.sin(angles)
+    cosine_wide = jnp.concatenate([cosine, cosine], axis=1)
+    sine_wide = jnp.concatenate([-sine, sine], axis=1)
 
     tokens_low = tokens.reshape(rows, width)
-    normed_low = rms_scale(tokens_low.astype(f32), gain_attn).astype(bf16)
-    proj = dot(normed_low, w_proj)
-    query_raw = proj[:, :q_cols]
-    key_raw = proj[:, q_cols : q_cols + k_cols]
-    value_raw = proj[:, q_cols + k_cols : q_cols + 2 * k_cols]
-    gate_raw = proj[:, q_cols + 2 * k_cols :]
+    ff = w_gate.shape[1]
+    (
+        normed_low,
+        query_raw,
+        kv_raw,
+        gate_raw,
+        queries,
+        kv_all,
+        attended,
+        lse,
+        gated_low,
+        normed_mlp_low,
+        resid_own,
+        wide_kvo,
+        wide_qg,
+        w_out_all,
+        wide_gate,
+        wide_up,
+        wide_down,
+        gain_wide,
+        gain_head,
+    ) = forward(
+        tokens_low,
+        cosine_wide,
+        sine_wide,
+        packs,
+        (w_gate, w_up, w_down.T),
+        scale,
+        seq_count,
+    )
+    key_raw = kv_raw[:, :k_cols]
+    gain_attn, gain_mlp = gain_wide[0:1], gain_wide[1:2]
+    gain_q, gain_k = gain_head[0], gain_head[1]
+    depth = w_gate.shape[0]
+    w_kvo = wide_kvo[:, :depth].reshape(width, -1)
+    w_qg = wide_qg.reshape(width, -1)
+    w_proj = jnp.concatenate([w_qg[:, :q_cols], w_kvo[:, : 2 * k_cols], w_qg[:, q_cols:]], axis=1)
+    proj_cols = w_proj.shape[1]
+    w_out_t = w_kvo[:, 2 * k_cols :]
+    wide_gate, wide_up, wide_down = (w.reshape(width, ff) for w in (wide_gate, wide_up, wide_down))
+    row_cosine = jnp.tile(cosine, (seq_count, 1))[:, None, :]
+    row_sine = jnp.tile(sine, (seq_count, 1))[:, None, :]
+    inputs_own = lax.dynamic_slice_in_dim(tokens_low, t * own_rows, own_rows, 0).astype(f32)
 
     def prepare(values, scales):
-        return head_prepare(values, scales, cosine, sine)
-
-    query_low = prepare(query_raw, gain_q).astype(bf16)
-    key_low = prepare(key_raw, gain_k).astype(bf16)
-    kv_own = jnp.concatenate([key_low, value_raw.astype(bf16)], axis=1)
-    (kv_all,) = batch_gather("keys_and_values", 2, kv_own)
+        return head_prepare(values, scales, row_cosine, row_sine)
 
     def by_head(values):
         shaped = values.reshape(seq_count, seq_dev, heads, head)
@@ -797,23 +1008,6 @@
     def by_row(values):
         shaped = values.reshape(seq_count, heads, seq_dev, head)
         return shaped.transpose(0, 2, 1, 3).reshape(rows, heads * head)
-
-    queries = by_head(query_low)
-    attended_heads, sums = attention_forward(queries, kv_all, scale)
-    attended = by_row(attended_heads)
-    lse = jnp.log2(sums[:, :, 0])[:, None, :]
-    gated_low = gate_apply(attended, gate_raw).astype(bf16)
-    attn_part = dot_t(gated_low, w_out_t).astype(bf16)
-
-    inputs_own = lax.dynamic_slice_in_dim(tokens_low, t * own_rows, own_rows, 0).astype(f32)
-    packs = (w_gate, w_up, w_down.T)
-    normed_mlp_low, resid_own, wide_gate, wide_up, wide_down = residual(
-        attn_part, inputs_own, gain_mlp, packs
-    )
-    ff = w_gate.shape[1]
-    wide_gate, wide_up, wide_down = (
-        w.reshape(width, ff) for w in (wide_gate, wide_up, wide_down)
-    )
 
     domain_range = jnp.arange(domain_counts.shape[0], dtype=jnp.int32)
     level_pick = (
@@ -859,7 +1053,7 @@
     grad_att_low = grad_attended.astype(bf16)
     grad_gate_raw_low = grad_gate_raw.astype(bf16)
     grad_att_heads = by_head(grad_att_low)
-    delta = jnp.sum(grad_att_heads.astype(f32) * attended_heads, axis=-1)[:, None, :]
+    delta = jnp.sum(grad_att_heads.astype(f32) * by_head(attended), axis=-1)[:, None, :]
     grad_query_heads, kv_part = attention_backward(
         queries, grad_att_heads, lse, delta, kv_all, scale
     )
@@ -898,7 +1092,7 @@
     def own_part(flat, like):
         return lax.dynamic_slice_in_dim(flat, b * like.shape[0], like.shape[0], 0)
 
-    pieces = [0, q_cols, q_cols + k_cols, q_cols + 2 * k_cols, proj_cols, pack_attn.shape[1]]
+    pieces = [0, q_cols, q_cols + k_cols, q_cols + 2 * k_cols, proj_cols, proj_cols + q_cols]
     grads = [attn_weight_grad[:, lo:hi] for lo, hi in zip(pieces[:-1], pieces[1:])]
     return (
         output.reshape(tokens.shape),

time: 505 us -> 467 us (0.925)
  Pallas kernels: 390 us -> 356 us
  other arithmetic: 37.3 us -> 26.1 us
  local copies, waits for them, and re-layouts: 20.8 us -> 29.8 us
    pallas_call x4 -> x1, Pallas kernels: 153 us -> 133 us  [forward(): pl.pallas_call(functools.partial(forward_kernel, scale), out_shape=[o for...]
    pallas_call x1, Pallas kernels: 76.5 us -> 69.9 us  [mlp_back(): pl.pallas_call(mlp_back_kernel, out_shape=[jax.ShapeDtypeStruct(part.shap...]
    dot_general x5 -> x4, matrix products: 15.9 us -> 12.9 us  [dot(): return jnp.dot(left, right, preferred_element_type=f32)]
    dot_general x5 -> x4, matrix products: 17.8 us -> 15.7 us  [dot_t(): lax.dot_general(left, right, (((1,), (1,)), ((), ())), preferred_element_...]
    unnamed x91 -> x93, local copies, waits for them, and re-layouts: 10.5 us -> 11.8 us
where the time goes in v2:
time: 467 us; the launch traced here: 459 us
  Pallas kernels  356 us (76%)
  matrix products  45.2 us (10%)
  local copies, waits for them, and re-layouts  29.8 us (6%)
  other arithmetic  26.1 us (6%)
    pallas_call x1, Pallas kernels, forward(): pl.pallas_call(functools.partial(forward_kernel, scale), out_shape=[o for...  133 us
    pallas_call x1, Pallas kernels, output_and_kv(): pl.pallas_call(output_kernel, out_shape=[jax.ShapeDtypeStruct(part.shape,...  74.3 us
    pallas_call x1, Pallas kernels, last_step(): pl.pallas_call(last_kernel, out_shape=[jax.ShapeDtypeStruct(part.shape, b...  70.3 us
    pallas_call x1, Pallas kernels, mlp_back(): pl.pallas_call(mlp_back_kernel, out_shape=[jax.ShapeDtypeStruct(part.shap...  69.9 us
    dot_general x5, matrix products, t_dot(): lax.dot_general(left, right, (((0,), (0,)), ((), ())), preferred_element_...  16.6 us
    dot_general x4, matrix products, dot_t(): lax.dot_general(left, right, (((1,), (1,)), ((), ())), preferred_element_...  15.7 us
    dot_general x4, matrix products, dot(): return jnp.dot(left, right, preferred_element_type=f32)  12.9 us
    unnamed x93, local copies, waits for them, and re-layouts  11.8 us

profile of v2, /device:TPU:1, one launch (start us, length us, event | category | flops | bytes accessed | tf_op | source)
XLA Modules:
  0.0 459.4 jit_solution(9778983755146071121)
XLA Ops:
  2.0 0.9 pad_maximum_fusion.5
  3.9 0.8 maximum_maximum_fusion
  4.6 0.9 copy.137
  5.6 1.5 fusion.27.pack_a
  7.0 1.5 pad_maximum_fusion.7.pack_b
  8.6 1.7 copy.138
  10.3 133.3 %forward.1 = (bf16[640,2048]{1,0:T(8,128)(2,1)}, f32[640,256]{1,0:T(8,128)}, f32[640,256]{1,0:T(8,128)}, f32[640,256]{1,0:T(8,128)}, bf16[2,640,128]{2,1,0:T(8,1...) custom-call(bf16[640,2048]{1,0:T(8,128)(2,1)} %bitcast.143, ...), custom_call_target="tpu_custom_call" | custom-call | tf_op jit(solution)/shard_map/forward/pallas_call | solution.py:559
  143.7 5.0 %fusion.41 = f32[640,768]{1,0:T(8,128)S(1)} fusion(bf16[640,2048]{1,0:T(8,128)(2,1)} %get-tuple-element.79, bf16[2048,768]{1,0:T(8,128)(2,1)} %bitcast.158), kind=kOutput, calls=%fused_computation.111 | convolution fusion | flops 2013265920 | bytes 7733248 | tf_op jit(solution)/shard_map/dot_general | solution.py:892
  148.8 2.2 fusion.42
  151.4 0.9 multiply_convert_fusion.1
  152.3 1.0 copy-done.28
  153.3 4.0 multiply_convert_fusion.3
  157.3 3.7 convolution_convert_fusion.5.part
  161.3 4.6 fusion.43
  165.9 3.9 add_convert_fusion.part
  170.1 1.0 convert_multiply_fusion.grad_final
  171.0 1.5 fusion.39
  172.6 4.9 %convolution_convert_fusion.1 = bf16[2048,768]{1,0:T(8,128)(2,1)S(1)} fusion(bf16[640,768]{1,0:T(8,128)(2,1)} %copy-done.41, bf16[640,2048]{1,0:T(8,128)(2,1)} %bitcast.141, f32[640]{0:T(1024)S(1)} %mul.307), kind=kOutput, calls=%fused_computation.6 | convolution fusion | flops 2018770944 | bytes 6752768 | tf_op jit(solution)/shard_map/dot_general | solution.py:900
  177.6 2.9 convolution_convert_fusion.2
  180.5 2.9 convolution_convert_fusion.3
  183.4 5.1 %pad_maximum_fusion.weight_part = bf16[2048,2304]{1,0:T(8,128)(2,1)} fusion(bf16[2048,768]{1,0:T(8,128)(2,1)S(1)} %convolution_convert_fusion.1, bf16[2048,768]{1,0:T(8,128)(2,1)S(1)} %convolution_convert_fusion.2, bf16[2048,768]{1,0:T(8,128)(2,1)S(1)} %convolution_convert_fusion.3), kind=kLoop, calls=%fused_computation | loop fusion | flops 28311552 | bytes 18874368 | tf_op jit(solution)/shard_map/concatenate | solution.py:1038
  188.5 69.9 %mlp_grad_and_weights.1 = (bf16[640,2048]{1,0:T(8,128)(2,1)}, f32[80,2048]{1,0:T(8,128)}, f32[1,2048]{1,0:T(1,128)}, f32[128,2304]{1,0:T(8,128)}) custom-call(bf16[640,2048]{1,0:T(8,128)(2,1)} %add_convert_fusion.part, f32[80,2048]{1,0:T(8,128)} %get-tuple-element.83.resid, f32[80,2048]{1,0:T(8,128)} %convert_multiply_fusion.grad_final, ...), custom_call_target="tpu_custom_call" | custom-call | tf_op jit(solution)/shard_map/mlp_grad_and_weights/pallas_call | solution.py:707
  258.6 0.8 copy-done.18
  259.5 1.6 copy-done.30
  261.2 1.6 fusion.14
  264.0 8.6 %attention_backward.1 = (f32[2,640,128]{2,1,0:T(8,128)S(1)}, bf16[16,640,256]{2,1,0:T(8,128)(2,1)}) custom-call(bf16[2,640,128]{2,1,0:T(8,128)(2,1)S(1)} %copy-done.1, bf16[2,128,640]{2,1,0:T(8,128)(2,1)S(1)} %bitcast.135, bf16[2,640,128]{2,1,0:T(8,128)(2,1)S(1)} %bitcast.132, bf16[2,128,640]{2,1,0:T(8,128)(2,1)S(1)} %bitcast.136, ...), custom_call_target="tpu_custom_call" | custom-call | tf_op jit(solution)/shard_map/attention_backward/pallas_call | solution.py:633
  272.6 74.3 %output_and_kv_grads.1 = (bf16[640,2048]{1,0:T(8,128)(2,1)S(1)}, f32[640,256]{1,0:T(8,128)S(1)}) custom-call(bf16[640,2048]{1,0:T(8,128)(2,1)} %convolution_convert_fusion.5.part, f32[80,2048]{1,0:T(8,128)S(1)} %copy-done, bf16[16,640,256]{2,1,0:T(8,128)(2,1)} %get-tuple-element.92.kv_part), custom_call_target="tpu_custom_call" | custom-call | tf_op jit(solution)/shard_map/output_and_kv_grads/pallas_call | solution.py:758
  346.9 1.5 fusion.37
  348.3 0.9 copy-done.8
  349.2 1.1 slice.146
  351.4 0.8 slice_bitcast_fusion.6
  352.5 1.0 fusion.26
  353.5 2.3 reshape.330
  355.7 2.6 multiply_reduce_fusion
  358.3 1.1 copy.148
  359.5 1.0 tile.22
  362.9 3.5 convolution_convert_fusion.4.part
  366.4 1.0 dynamic-slice_convert_fusion.inputs
  367.9 2.9 convolution_convert_fusion.6
  370.9 2.9 convolution_convert_fusion
  373.8 2.6 pad_maximum_fusion.1.weight_part
  376.4 70.3 %input_grad_and_weights.1 = (bf16[640,2048]{1,0:T(8,128)(2,1)S(1)}, f32[128,1024]{1,0:T(8,128)S(1)}, f32[40,128]{1,0:T(8,128)S(1)}) custom-call(bf16[640,2048]{1,0:T(8,128)(2,1)} %convolution_convert_fusion.4.part, f32[80,2048]{1,0:T(8,128)S(1)} %dynamic-slice_convert_fusion.inputs, f32[80,2048]{1,0:T(8,128)S(1)} %copy-done.2, ...), custom_call_target="tpu_custom_call" | custom-call | tf_op jit(solution)/shard_map/input_grad_and_weights/pallas_call | solution.py:838
  446.8 3.0 convert.5
  449.8 0.7 slice_bitcast_fusion.2
  451.2 0.8 copy.156
  452.0 2.2 slice_bitcast_fusion
  454.1 0.9 copy.157
  457.4 1.5 copy.179
  (131 shorter events, 11.9 us)
Async XLA Ops:
  1.3 0.7 copy-start.10
  143.7 5.0 %copy-start.26 = (bf16[16,128,768]{2,1,0:T(8,128)(2,1)S(1)}, bf16[16,128,768]{2,1,0:T(8,128)(2,1)}, u32[]{:S(2)}) copy-start(bf16[16,128,768]{2,1,0:T(8,128)(2,1)} %get-tuple-element.81) | copy-start | bytes 9437188
  143.7 5.0 %copy-start.31 = (bf16[640,2048]{1,0:T(8,128)(2,1)S(1)}, bf16[640,2048]{1,0:T(8,128)(2,1)}, u32[]{:S(2)}) copy-start(bf16[640,2048]{1,0:T(8,128)(2,1)} %get-tuple-element.79) | copy-start | bytes 7864324
  148.7 2.3 copy-start.34
  148.7 2.3 copy-start.35
  148.7 2.4 copy-start.36
  148.8 2.4 copy-start.37
  148.8 2.6 copy-start.9
  151.4 1.9 copy-start.28
  157.3 3.7 copy-start.41
  157.3 3.7 copy-start.1
  161.3 4.6 copy-start.27
  161.3 4.6 copy-start.39
  172.6 4.9 %copy-start.32 = (bf16[640,2048]{1,0:T(8,128)(2,1)S(1)}, bf16[640,2048]{1,0:T(8,128)(2,1)}, u32[]{:S(2)}) copy-start(bf16[640,2048]{1,0:T(8,128)(2,1)} %get-tuple-element.79) | copy-start | bytes 7864324
  172.6 5.0 %copy-start.40 = (bf16[640,768]{1,0:T(8,128)(2,1)S(1)}, bf16[640,768]{1,0:T(8,128)(2,1)}, u32[]{:S(2)}) copy-start(bf16[640,768]{1,0:T(8,128)(2,1)} %get-tuple-element.196) | copy-start | bytes 2949124
  177.6 2.9 copy-start.38
  188.5 69.9 %copy-start.13 = (bf16[16,144,512]{2,1,0:T(8,128)(2,1)S(1)}, bf16[16,144,512]{2,1,0:T(8,128)(2,1)}, u32[]{:S(2)}) copy-start(bf16[16,144,512]{2,1,0:T(8,128)(2,1)} %get-tuple-element.87) | copy-start | bytes 7077892
  258.4 1.1 copy-start.18
  258.4 2.7 copy-start.30
  258.4 2.8 copy-start.33
  258.6 4.2 copy-start.7
  262.9 1.1 copy-start.5
  264.0 8.6 %copy-start = (f32[80,2048]{1,0:T(8,128)S(1)}, f32[80,2048]{1,0:T(8,128)}, u32[]{:S(2)}) copy-start(f32[80,2048]{1,0:T(8,128)} %get-tuple-element.83.resid) | copy-start | bytes 1966084
  272.6 74.3 %copy-start.3 = (f32[2,640,128]{2,1,0:T(8,128)}, f32[2,640,128]{2,1,0:T(8,128)S(1)}, u32[]{:S(2)}) copy-start(f32[2,640,128]{2,1,0:T(8,128)S(1)} %get-tuple-element.94) | copy-start | bytes 1966084
  272.6 74.3 %copy-start.12 = (bf16[16,128,512]{2,1,0:T(8,128)(2,1)S(1)}, bf16[16,128,512]{2,1,0:T(8,128)(2,1)}, u32[]{:S(2)}) copy-start(bf16[16,128,512]{2,1,0:T(8,128)(2,1)} %get-tuple-element.99) | copy-start | bytes 6291460
  346.9 2.3 copy-start.8
  346.9 4.1 copy-start.14
  348.3 2.8 copy-start.11
  351.4 8.1 %copy-start.4 = (f32[2,640,128]{2,1,0:T(8,128)S(1)}, f32[2,640,128]{2,1,0:T(8,128)}, u32[]{:S(2)}) copy-start(f32[2,640,128]{2,1,0:T(8,128)} %copy-done.3) | copy-start | bytes 1966084
  359.5 1.5 copy-start.6
  360.9 1.3 copy-start.15
  360.9 1.5 copy-start.16
  360.9 1.8 copy-start.17
  360.9 1.8 copy-start.21
  360.9 1.9 copy-start.23
  360.9 2.0 copy-start.42
  362.9 3.5 copy-start.19
  362.9 4.5 copy-start.25
  367.8 3.0 copy-start.20
  367.8 3.0 copy-start.22
  367.9 3.0 copy-start.24
  367.9 3.0 copy-start.29
  367.9 3.0 copy-start.43
  373.8 2.6 copy-start.2
